TPU v7x, 32 devices: a whole 2x2x4 slice. The times are simulated.
32 devices in a mesh: dp: 16 (over z, y, x), fsdp: 2 (over core).
Axes of the slice: x: 2, y: 2, z: 4, core: 2. Of those that a mesh axis runs over, the one named last changes fastest.
Arguments:
- query_emb: bfloat16 [8192, 4096], P('dp', 'fsdp')
- passage_emb: bfloat16 [16384, 4096], P('dp', 'fsdp')
- cand_blocks: int32 [64, 4], P('dp'), may hold values from 0 to 127, as said below
- positive: int32 [8192], P('dp'), may hold values from 0 to 511
Outputs:
- losses: float32 [8192], P(('dp', 'fsdp'))
- query_grad: bfloat16 [8192, 4096], P('dp', 'fsdp')
Inputs may be any that keep to these rules, and one draw needn't show every extreme that they name: `cand_blocks`: each query block lists 4 different passage blocks; block b is held by dp index b // 8. The blocks listed by the 4 query blocks of one dp index are all different, at most 1 of them are held by any one dp index, and some dp index holds exactly 1 of them. `positive`: position c names row c % 128 of the block in column c // 128 of the query's list.
All inputs are finite; a program needn't handle non-finite values.
Results may differ from a plain program's by a relative error of at most 0.0038.
Values may be sent and summed in bfloat16 or wider, within the bound.
No kernel may reach another device: no remote copies, remote signals or barrier semaphores. Data moves between devices by JAX's collectives and lax.ppermute only.
A program may use at most 64 MiB of HBM per device.

v0:
```python
import jax
import jax.numpy as jnp
from jax import lax
from jax.sharding import PartitionSpec as P


def softmax_rows(scores, positive_rows):
    row_max = jnp.max(scores, axis=1, keepdims=True)
    log_total = row_max[:, 0] + jnp.log(jnp.sum(jnp.exp(scores - row_max), axis=1))
    matched = lax.broadcasted_iota(jnp.int32, scores.shape, 1) == positive_rows[:, None]
    losses = log_total - jnp.sum(jnp.where(matched, scores, jnp.float32(0.0)), axis=1)
    weights = (jnp.exp(scores - log_total[:, None]) - matched.astype(jnp.float32)).astype(
        jnp.bfloat16
    )
    return (losses, weights)


def slot_ranks(owners):
    length = owners.shape[-1]
    same_owner = owners[..., :, None] == owners[..., None, :]
    earlier = lax.broadcasted_iota(jnp.int32, (length, length), 1) < lax.broadcasted_iota(
        jnp.int32, (length, length), 0
    )
    return jnp.sum((same_owner & earlier).astype(jnp.int32), axis=-1)


def shards(query_emb, passage_emb, cand_blocks, positive):
    dp_count = lax.axis_size("dp")
    fsdp_count = lax.axis_size("fsdp")
    query_blocks, list_len = cand_blocks.shape
    row_count, feature_count = query_emb.shape
    block_rows = row_count // query_blocks
    passage_blocks = passage_emb.shape[0] // block_rows
    capacity = (list_len * query_blocks + dp_count - 1) // dp_count
    slot_count = dp_count * capacity
    wanted = cand_blocks.reshape(-1)
    owners = wanted // passage_blocks
    local_ids = wanted % passage_blocks
    placed = owners * capacity + slot_ranks(owners)
    matched = lax.broadcasted_iota(jnp.int32, (slot_count, wanted.shape[0]), 0) == placed[None, :]
    id_table = jnp.sum(jnp.where(matched, local_ids[None, :], 0), axis=1).reshape(
        dp_count, capacity
    )
    requested = lax.all_to_all(id_table, "dp", split_axis=0, concat_axis=0, tiled=True)
    stored = passage_emb.reshape(passage_blocks, block_rows, feature_count)
    outgoing = stored[requested]
    fetched = lax.all_to_all(outgoing, "dp", split_axis=0, concat_axis=0, tiled=True)
    candidates = fetched.reshape(slot_count, block_rows, feature_count)[placed]
    candidates = candidates.reshape(query_blocks, list_len * block_rows, feature_count)
    query_rows = query_emb.reshape(query_blocks, block_rows, feature_count)
    partial_value = jnp.einsum(
        "qnd,qcd->qnc", query_rows, candidates, preferred_element_type=jnp.float32
    )
    partial_value = partial_value.reshape(row_count, list_len * block_rows)
    share_rows = row_count // fsdp_count
    first_row = lax.axis_index("fsdp") * share_rows
    scores = lax.psum_scatter(partial_value, "fsdp", scatter_dimension=0, tiled=True) * 50.0
    losses, part_weights = softmax_rows(
        scores, lax.dynamic_slice_in_dim(positive, first_row, share_rows)
    )
    weights = lax.all_gather(part_weights, "fsdp", axis=0, tiled=True)
    weights = weights.reshape(query_blocks, block_rows, list_len * block_rows)
    query_grad = (
        jnp.einsum("qnc,qcd->qnd", weights, candidates, preferred_element_type=jnp.float32) * 50.0
    )
    return (losses, query_grad.astype(jnp.bfloat16).reshape(row_count, feature_count))


def solution(mesh):
    return jax.shard_map(
        shards,
        mesh=mesh,
        in_specs=(P("dp", "fsdp"), P("dp", "fsdp"), P("dp", None), P("dp")),
        out_specs=(P(("dp", "fsdp")), P("dp", "fsdp")),
        check_vma=False,
    )
```

profile of v0, /device:TPU:11, one launch (start us, length us, event | category | flops | bytes accessed | tf_op | source)
XLA Modules:
  0.0 266.2 jit_solution(685318356553481967)
XLA Ops:
  7.2 0.0 copy-start
  7.2 0.9 reshape.208
  8.1 0.2 convert_reduce_fusion
  8.3 0.1 select_reduce_fusion.1
  8.4 0.1 copy.8
  8.5 10.6 %all_to_all.14 = s32[16,1,1]{2,1,0:T(1,128)S(1)} all-to-all(s32[16,1,1]{2,1,0:T(1,128)S(1)} %copy.8), channel_id=1, replica_groups=mesh['dp'=16,'fsdp'=2] {'dp'}, dimensions={0} | all-to-all | bytes 128 | tf_op jit(solution)/shard_map/all_to_all | solution.py:44
  19.1 0.4 fusion
  19.5 7.0 %gather_fusion = bf16[16,128,2048]{2,1,0:T(8,128)(2,1)} fusion(bf16[8,128,2048]{2,1,0:T(8,128)(2,1)} %bitcast.25, s32[1024]{0:T(1024)S(1)} %pad_clamp_fusion.1), kind=kCustom, calls=%fused_computation | custom fusion | bytes 16777280 | tf_op jit(solution)/shard_map/gather | solution.py:46
  26.4 0.0 copy-start.1
  26.4 6.7 %all-to-all-start.1 = ((bf16[16,1,128,2048]{3,2,1,0:T(8,128)(2,1)}), bf16[16,1,128,2048]{3,2,1,0:T(8,128)(2,1)}, u32[]{:S(2)}, u32[]{:S(2)}) async-start(bf16[16,1,128,2048]{3,2,1,0:T(8,128)(2,1)} %bitcast.24), calls=%async_computation.1 | async-start | bytes 16777216 | tf_op jit(solution)/shard_map/all_to_all | solution.py:47
  33.1 0.0 reduce-scatter.2.cloned.1.call-start
  33.2 0.0 copy-done.1
  33.2 0.1 reshape.210
  33.3 184.4 %all-to-all-done.1 = bf16[16,1,128,2048]{3,2,1,0:T(8,128)(2,1)} async-done(((bf16[16,1,128,2048]{3,2,1,0:T(8,128)(2,1)}), bf16[16,1,128,2048]{3,2,1,0:T(8,128)(2,1)}, u32[]{:S(2)}, u32[]{:S(2)}) %all-to-all-start.1) | async-done | bytes 8388640 | tf_op jit(solution)/shard_map/all_to_all | solution.py:47
  217.7 8.1 %gather_fusion.1 = bf16[16,128,2048]{2,1,0:T(8,128)(2,1)} fusion(bf16[16,128,2048]{2,1,0:T(8,128)(2,1)} %bitcast.3, s32[1024]{0:T(1024)S(1)} %pad_clamp_fusion), kind=kCustom, calls=%fused_computation.1 | custom fusion | bytes 16777280 | tf_op jit(solution)/shard_map/gather | solution.py:48
  225.9 0.0 copy-start.2
  225.9 0.0 copy-done
  225.9 7.3 %fusion.4 = f32[4,512,128]{1,2,0:T(8,128)} fusion(bf16[4,512,2048]{2,1,0:T(8,128)(2,1)} %bitcast.22, bf16[4,128,2048]{2,1,0:T(8,128)(2,1)S(1)} %bitcast.21), kind=kOutput, calls=%fused_computation.31 | convolution fusion | flops 1073741824 | bytes 11534336 | tf_op jit(solution)/shard_map/qnd,qcd->qnc/dot_general | solution.py:51
  233.2 0.0 reduce-scatter.2.cloned.1.call-update
  233.2 0.0 copy-done.2
  233.2 0.1 dynamic_slice.3
  233.3 13.6 %reduce-scatter.2.cloned.1.call-done = f32[256,512]{1,0:T(8,128)} async-done(((f32[512,512]{1,0:T(8,128)}), f32[256,512]{1,0:T(8,128)}) %reduce-scatter.2.cloned.1.call-update) | async-done | bytes 524304 | tf_op jit(solution)/shard_map/reduce_scatter | solution.py:57
  246.9 1.2 multiply_reduce_fusion
  248.0 1.4 select_reduce_fusion
  249.4 0.6 fusion.3
  250.0 1.2 subtract_convert_fusion
  251.2 2.2 all_gather.3
  253.4 6.0 %multiply_convert_fusion = bf16[4,128,2048]{2,1,0:T(8,128)(2,1)} fusion(bf16[4,128,512]{2,1,0:T(8,128)(2,1)S(1)} %bitcast.27, bf16[4,512,2048]{2,1,0:T(8,128)(2,1)} %bitcast.23), kind=kOutput, calls=%fused_computation.2 | convolution fusion | flops 1075838976 | bytes 11010048 | tf_op jit(solution)/shard_map/qnc,qcd->qnd/dot_general | solution.py:64
  (5 shorter events, 0.1 us)
Async XLA Ops:
  7.2 218.7 %copy-start = (bf16[512,2048]{1,0:T(8,128)(2,1)S(1)}, bf16[512,2048]{1,0:T(8,128)(2,1)}, u32[]{:S(2)}) copy-start(bf16[512,2048]{1,0:T(8,128)(2,1)} %param.4) | copy-start | bytes 6291460
  26.4 6.8 %copy-start.1 = (s32[4,4]{1,0:T(4,128)S(1)}, s32[4,4]{1,0:T(4,128)}, u32[]{:S(2)}) copy-start(s32[4,4]{1,0:T(4,128)} %param.6) | copy-start | bytes 196
  26.4 191.3 %all-to-all-start.1 = ((bf16[16,1,128,2048]{3,2,1,0:T(8,128)(2,1)}), bf16[16,1,128,2048]{3,2,1,0:T(8,128)(2,1)}, u32[]{:S(2)}, u32[]{:S(2)}) async-start(bf16[16,1,128,2048]{3,2,1,0:T(8,128)(2,1)} %bitcast.24), calls=%async_computation.1 | async-start | bytes 16777216 | tf_op jit(solution)/shard_map/all_to_all | solution.py:47
  33.1 213.7 %reduce-scatter.2.cloned.1.call-start = ((), (), s32[]{:S(2)}) async-start(), calls=%async_computation.3 | async-start | bytes 1572864 | tf_op jit(solution)/shard_map/reduce_scatter | solution.py:57
  225.9 7.3 %copy-start.2 = (s32[512]{0:T(512)S(1)}, s32[512]{0:T(512)}, u32[]{:S(2)}) copy-start(s32[512]{0:T(512)} %param.7) | copy-start | bytes 6148
Sparse Core Ops, SparseCore 0:
  233.3 13.4 reduce-scatter.1
where the time goes:
time: 268 us; the launch traced here: 266 us
  waiting for transfers between devices  198 us (74%)
  local copies, waits for them, and re-layouts  16.3 us (6%)
  between operations  14.1 us (5%)
  matrix products  13.3 us (5%)
  blocking collectives  12.8 us (5%)
  starting transfers between devices  6.75 us (3%)
  other arithmetic  5.09 us (2%)
    all_to_all x1, waiting for transfers between devices, shards(): lax.all_to_all(outgoing, 'dp', split_axis=0, concat_axis=0, tiled=True)  184 us
    reduce_scatter x1, waiting for transfers between devices, shards(): lax.psum_scatter(partial_value, 'fsdp', scatter_dimension=0, tiled=True)  13.6 us
    all_to_all x1, blocking collectives, shards(): lax.all_to_all(id_table, 'dp', split_axis=0, concat_axis=0, tiled=True)  10.6 us
    gather x1, local copies, waits for them, and re-layouts, shards(): candidates = fetched.reshape(slot_count, block_rows, feature_count)[placed]  8.14 us
    dot_general x1, matrix products, shards(): jnp.einsum('qnd,qcd->qnc', query_rows, candidates, preferred_element_type...  7.29 us
    gather x1, local copies, waits for them, and re-layouts, shards(): outgoing = stored[requested]  6.95 us
    all_to_all x1, starting transfers between devices, shards(): lax.all_to_all(outgoing, 'dp', split_axis=0, concat_axis=0, tiled=True)  6.72 us
    dot_general x1, matrix products, shards(): jnp.einsum('qnc,qcd->qnd', weights, candidates, preferred_element_type=jn...  5.97 us
  transfers between devices with their start and end apart: 2, of which 2 were waited for; matrix products, arithmetic and copies ran while one was open for 0% of the time, Pallas kernels for 0%

commit v1 on v0

v1 whole, which is shorter than its diff:
```python
import functools

import jax
import jax.numpy as jnp
from jax import lax
from jax.experimental import pallas as pl
from jax.experimental.pallas import tpu as pltpu
from jax.sharding import PartitionSpec as P

VMEM_LIMIT = 48 * 1024 * 1024
TILE = 512


def listed(slots_ref, block_ref, query_block, list_len):
    return jnp.concatenate(
        [block_ref[slots_ref[query_block, j]] for j in range(list_len)], axis=0
    )


def score_kernel(slots_ref, query_ref, block_ref, out_ref):
    query_blocks, list_len = slots_ref.shape
    block_rows = block_ref.shape[1]
    step = pl.program_id(0)
    for b in range(query_blocks):
        rows = pl.ds(b * block_rows, block_rows)
        share = lax.dot_general(
            query_ref[rows, :],
            listed(slots_ref, block_ref, b, list_len),
            (((1,), (1,)), ((), ())),
            preferred_element_type=jnp.float32,
        )

        @pl.when(step == 0)
        def _():
            out_ref[rows, :] = share

        @pl.when(step > 0)
        def _():
            out_ref[rows, :] += share


def partial_scores(slots, query_emb, blocks):
    query_blocks, list_len = slots.shape
    slot_count, block_rows, features = blocks.shape
    rows = query_emb.shape[0]
    tile = min(TILE, features)
    columns = list_len * block_rows
    return pl.pallas_call(
        score_kernel,
        out_shape=jax.ShapeDtypeStruct((rows, columns), jnp.float32),
        grid_spec=pltpu.PrefetchScalarGridSpec(
            num_scalar_prefetch=1,
            grid=(features // tile,),
            in_specs=[
                pl.BlockSpec((rows, tile), lambda t, s: (0, t)),
                pl.BlockSpec((slot_count, block_rows, tile), lambda t, s: (0, 0, t)),
            ],
            out_specs=pl.BlockSpec((rows, columns), lambda t, s: (0, 0)),
        ),
        compiler_params=pltpu.CompilerParams(vmem_limit_bytes=VMEM_LIMIT),
        cost_estimate=pl.CostEstimate(
            flops=2 * rows * columns * features,
            bytes_accessed=2 * blocks.size + 2 * query_emb.size + 4 * rows * columns,
            transcendentals=0,
        ),
        name="partial_scores",
    )(slots, query_emb, blocks)


def gradient_kernel(
    share_count, slots_ref, first_ref, positive_ref, *refs
):
    share_refs = refs[:share_count]
    block_ref, loss_ref, grad_ref, weight_ref, all_loss_ref = refs[share_count:]
    query_blocks, list_len = slots_ref.shape
    block_rows = block_ref.shape[1]

    @pl.when(pl.program_id(0) == 0)
    def _():
        for b in range(query_blocks):
            rows = pl.ds(b * block_rows, block_rows)
            total = share_refs[0][rows, :]
            for ref in share_refs[1:]:
                total = total + ref[rows, :]
            scores = total * 50.0
            row_max = jnp.max(scores, axis=1, keepdims=True)
            log_total = row_max + jnp.log(
                jnp.sum(jnp.exp(scores - row_max), axis=1, keepdims=True)
            )
            matched = (
                lax.broadcasted_iota(jnp.int32, scores.shape, 1) == positive_ref[rows, :]
            )
            picked = jnp.sum(jnp.where(matched, scores, 0.0), axis=1, keepdims=True)
            all_loss_ref[rows, :] = log_total - picked
            weight_ref[rows, :] = (
                jnp.exp(scores - log_total) - matched.astype(jnp.float32)
            ).astype(jnp.bfloat16)
        loss_ref[...] = all_loss_ref[pl.ds(first_ref[0], loss_ref.shape[0]), :]

    for b in range(query_blocks):
        rows = pl.ds(b * block_rows, block_rows)
        grad = jnp.dot(
            weight_ref[rows, :],
            listed(slots_ref, block_ref, b, list_len),
            preferred_element_type=jnp.float32,
        )
        grad_ref[rows, :] = (grad * 50.0).astype(jnp.bfloat16)


def losses_and_gradients(slots, first_row, share_rows, positive, shares, blocks):
    slot_count, block_rows, features = blocks.shape
    rows, columns = shares[0].shape
    tile = min(TILE, features)
    whole = lambda t, s, f: (0, 0)
    return pl.pallas_call(
        functools.partial(gradient_kernel, len(shares)),
        out_shape=(
            jax.ShapeDtypeStruct((share_rows, 1), jnp.float32),
            jax.ShapeDtypeStruct((rows, features), jnp.bfloat16),
        ),
        grid_spec=pltpu.PrefetchScalarGridSpec(
            num_scalar_prefetch=2,
            grid=(features // tile,),
            in_specs=[pl.BlockSpec((rows, 1), whole)]
            + [pl.BlockSpec((rows, columns), whole)] * len(shares)
            + [pl.BlockSpec((slot_count, block_rows, tile), lambda t, s, f: (0, 0, t))],
            out_specs=[
                pl.BlockSpec((share_rows, 1), whole),
                pl.BlockSpec((rows, tile), lambda t, s, f: (0, t)),
            ],
            scratch_shapes=[
                pltpu.VMEM((rows, columns), jnp.bfloat16),
                pltpu.VMEM((rows, 1), jnp.float32),
            ],
        ),
        compiler_params=pltpu.CompilerParams(vmem_limit_bytes=VMEM_LIMIT),
        cost_estimate=pl.CostEstimate(
            flops=2 * rows * columns * features,
            bytes_accessed=2 * blocks.size + 2 * rows * features + 8 * rows * columns,
            transcendentals=2 * rows * columns,
        ),
        name="losses_and_gradients",
    )(slots, first_row, positive.reshape(rows, 1), *shares, blocks)


def shards(query_emb, passage_emb, cand_blocks, positive):
    dp_count = lax.axis_size("dp")
    fsdp_count = lax.axis_size("fsdp")
    query_blocks, list_len = cand_blocks.shape
    row_count, feature_count = query_emb.shape
    block_rows = row_count // query_blocks
    passage_blocks = passage_emb.shape[0] // block_rows
    owners = cand_blocks // passage_blocks
    local_ids = cand_blocks % passage_blocks
    owner_index = lax.broadcasted_iota(jnp.int32, (dp_count, query_blocks, list_len), 0)
    id_table = jnp.sum(jnp.where(owner_index == owners[None], local_ids[None], 0), axis=(1, 2))
    requested = lax.all_to_all(
        id_table.reshape(dp_count, 1), "dp", split_axis=0, concat_axis=0, tiled=True
    ).reshape(dp_count)
    stored = passage_emb.reshape(passage_blocks, block_rows, feature_count)
    fetched = lax.all_to_all(stored[requested], "dp", split_axis=0, concat_axis=0, tiled=True)
    mine = partial_scores(owners, query_emb, fetched)
    shares = [mine] + [
        lax.ppermute(mine, "fsdp", [(i, (i + k) % fsdp_count) for i in range(fsdp_count)])
        for k in range(1, fsdp_count)
    ]
    share_rows = row_count // fsdp_count
    first_row = (lax.axis_index("fsdp") * share_rows).astype(jnp.int32).reshape(1)
    losses, query_grad = losses_and_gradients(
        owners, first_row, share_rows, positive, shares, fetched
    )
    return losses.reshape(share_rows), query_grad


def solution(mesh):
    return jax.shard_map(
        shards,
        mesh=mesh,
        in_specs=(P("dp", "fsdp"), P("dp", "fsdp"), P("dp", None), P("dp")),
        out_specs=(P(("dp", "fsdp")), P("dp", "fsdp")),
        check_vma=False,
    )
```

time: 268 us -> 231 us (0.86)
  waiting for transfers between devices: 198 us -> 2.13 us
  blocking collectives: 12.8 us -> 198 us
  Pallas kernels: 0 us -> 15.6 us
  between operations: 14.1 us -> 0.67 us
  matrix products: 13.3 us -> 0 us
  local copies, waits for them, and re-layouts: 16.3 us -> 7.19 us
  starting transfers between devices: 6.75 us -> 2.68 us
  other arithmetic: 5.09 us -> 1.85 us
    all_to_all x1 -> x2, blocking collectives: 10.6 us -> 198 us  [the longest x1 188 us: shards(): lax.all_to_all(stored[requested], 'dp', split_axis=0, concat_axis=0, tile...]
    all_to_all x1 -> x0, waiting for transfers between devices: 184 us -> none  [shards(): lax.all_to_all(outgoing, 'dp', split_axis=0, concat_axis=0, tiled=True)]
    pallas_call x0 -> x2, Pallas kernels: none -> 15.6 us  [the longest x1 7.85 us: partial_scores(): pl.pallas_call(score_kernel, out_shape=jax.ShapeDtypeStruct((rows, column...]
    reduce_scatter x1 -> x0, waiting for transfers between devices: 13.6 us -> none  [shards(): lax.psum_scatter(partial_value, 'fsdp', scatter_dimension=0, tiled=True)]
    dot_general x2 -> x0, matrix products: 13.3 us -> none  [the longest x1 7.29 us: shards(): jnp.einsum('qnd,qcd->qnc', query_rows, candidates, preferred_element_type...]
    gather x2 -> x1, local copies, waits for them, and re-layouts: 15.1 us -> 6.95 us  [shards(): stored[requested]]
    all_to_all x1 -> x0, starting transfers between devices: 6.72 us -> none  [shards(): lax.all_to_all(outgoing, 'dp', split_axis=0, concat_axis=0, tiled=True)]
    ppermute x0 -> x1, starting transfers between devices: none -> 2.68 us  [shards(): lax.ppermute(mine, 'fsdp', [(i, (i + k) % fsdp_count) for i in range(fsdp...]
  transfers between devices with their start and end apart: 2 -> 1, of which waited for: 2 -> 1; matrix products, arithmetic and copies ran while one was open for 0% -> 0% of each run, Pallas kernels for 0% -> 0%
where the time goes in v1:
time: 231 us; the launch traced here: 228 us
  blocking collectives  198 us (86%)
  Pallas kernels  15.6 us (7%)
  local copies, waits for them, and re-layouts  7.19 us (3%)
  starting transfers between devices  2.68 us (1%)
    all_to_all x1, blocking collectives, shards(): lax.all_to_all(stored[requested], 'dp', split_axis=0, concat_axis=0, tile...  188 us
    all_to_all x1, blocking collectives, shards(): lax.all_to_all(id_table.reshape(dp_count, 1), 'dp', split_axis=0, concat_...  10.6 us
    pallas_call x1, Pallas kernels, partial_scores(): pl.pallas_call(score_kernel, out_shape=jax.ShapeDtypeStruct((rows, column...  7.85 us
    pallas_call x1, Pallas kernels, losses_and_gradients(): pl.pallas_call(functools.partial(gradient_kernel, len(shares)), out_shape...  7.72 us
    gather x1, local copies, waits for them, and re-layouts, shards(): stored[requested]  6.95 us
  transfers between devices with their start and end apart: 1, of which 1 were waited for; matrix products, arithmetic and copies ran while one was open for 0% of the time, Pallas kernels for 0%

profile of v1, /device:TPU:11, one launch (start us, length us, event | category | flops | bytes accessed | tf_op | source)
XLA Modules:
  0.0 228.4 jit_solution(13561232026643863609)
XLA Ops:
  0.6 0.7 add_select_fusion
  1.3 0.1 select_reduce_fusion
  1.4 0.1 copy.11
  1.5 10.6 %all_to_all.17 = s32[16,1,1]{2,1,0:T(1,128)S(1)} all-to-all(s32[16,1,1]{2,1,0:T(1,128)S(1)} %copy.11), channel_id=1, replica_groups=mesh['dp'=16,'fsdp'=2] {'dp'}, dimensions={0} | all-to-all | bytes 128 | tf_op jit(solution)/shard_map/all_to_all | solution.py:157
  12.1 0.4 reduce
  12.5 7.0 %gather_fusion = bf16[16,128,2048]{2,1,0:T(8,128)(2,1)} fusion(bf16[8,128,2048]{2,1,0:T(8,128)(2,1)} %bitcast.8, s32[1024]{0:T(1024)S(1)} %pad_clamp_fusion), kind=kCustom, calls=%fused_computation | custom fusion | bytes 16777280 | tf_op jit(solution)/shard_map/gather | solution.py:161
  19.4 0.0 copy-start
  19.4 187.7 %all_to_all.18.block_ref.refs_2_ = bf16[16,128,2048]{2,1,0:T(8,128)(2,1)} all-to-all(bf16[16,128,2048]{2,1,0:T(8,128)(2,1)} %gather_fusion), channel_id=1, replica_groups=mesh['dp'=16,'fsdp'=2] {'dp'}, dimensions={0} | all-to-all | bytes 16777216 | tf_op jit(solution)/shard_map/all_to_all | solution.py:161
  207.1 0.0 copy-done
  207.1 0.0 copy-start.1
  207.2 7.9 %partial_scores.1.refs_0_ = f32[512,512]{1,0:T(8,128)S(1)} custom-call(s32[4,4]{1,0:T(4,128)S(1)} %get-tuple-element.7.slots_ref, bf16[512,2048]{1,0:T(8,128)(2,1)S(1)} %copy-done, bf16[16,128,2048]{2,1,0:T(8,128)(2,1)} %all_to_all.18.block_ref.refs_2_), custom_call_target="tpu_custom_call" | custom-call | flops 1073741824 | bytes 11534336 | tf_op jit(solution)/shard_map/partial_scores/pallas_call | solution.py:48
  215.0 2.7 %collective-permute-start = (f32[512,512]{1,0:T(8,128)S(1)}, f32[512,512]{1,0:T(8,128)S(1)}, u32[]{:S(2)}, u32[]{:S(2)}) collective-permute-start(f32[512,512]{1,0:T(8,128)S(1)} %partial_scores.1.refs_0_), channel_id=1, source_target_pairs={{0,1},{1,0},{2,3},{3,2},{4,5},{5,4},{6,7},{7,6},{8,9},{9,8},{10,11... | collective-permute-start | bytes 3145736 | tf_op jit(solution)/shard_map/ppermute | solution.py:164
  217.7 0.0 copy-done.1
  217.7 0.1 copy.12.positive_ref
  217.9 2.1 collective-permute-done.refs_1_
  220.0 7.7 %losses_and_gradients.1 = (f32[256,1]{1,0:T(8,128)S(1)}, bf16[512,2048]{1,0:T(8,128)(2,1)}) custom-call(s32[4,4]{1,0:T(4,128)S(1)} %get-tuple-element.7.slots_ref, s32[1]{0:T(128)} %bitcast.first_ref, s32[512,1]{1,0:T(8,128)S(1)} %copy.12.positive_ref, f32[512,512]{1,0:T(8,128)S(1)} %partial_scores.1.refs_0_, f32[512,512]{1,0:T(8,128)S(1)} %collective-permute-done.refs_1_, ...), custom_call_target="tpu_custom_call" | custom-call | flops 1073741824 | bytes 12582912 | tf_op jit(solution)/shard_map/losses_and_gradients/pallas_call | solution.py:115
  227.7 0.7 reduce.1
  (2 shorter events, 0.0 us)
Async XLA Ops:
  19.4 187.7 %copy-start = (bf16[512,2048]{1,0:T(8,128)(2,1)S(1)}, bf16[512,2048]{1,0:T(8,128)(2,1)}, u32[]{:S(2)}) copy-start(bf16[512,2048]{1,0:T(8,128)(2,1)} %query_ref.1) | copy-start | bytes 6291460
  207.1 10.5 %copy-start.1 = (s32[512]{0:T(512)S(1)}, s32[512]{0:T(512)}, u32[]{:S(2)}) copy-start(s32[512]{0:T(512)} %param.7) | copy-start | bytes 6148
  215.0 5.0 %collective-permute-start = (f32[512,512]{1,0:T(8,128)S(1)}, f32[512,512]{1,0:T(8,128)S(1)}, u32[]{:S(2)}, u32[]{:S(2)}) collective-permute-start(f32[512,512]{1,0:T(8,128)S(1)} %partial_scores.1.refs_0_), channel_id=1, source_target_pairs={{0,1},{1,0},{2,3},{3,2},{4,5},{5,4},{6,7},{7,6},{8,9},{9,8},{10,11... | collective-permute-start | bytes 3145736 | tf_op jit(solution)/shard_map/ppermute | solution.py:164

commit v2 on v0

v2 whole, which is shorter than its diff:
```python
import functools

import jax
import jax.numpy as jnp
from jax import lax
from jax.experimental import pallas as pl
from jax.experimental.pallas import tpu as pltpu
from jax.sharding import PartitionSpec as P

VMEM_LIMIT = 32 * 1024 * 1024
TILE = 512
LANES = 128
WINDOW = 8
SHIFT = 1 << 16
IN_VMEM = pl.BlockSpec(memory_space=pltpu.VMEM)
IN_HBM = pl.BlockSpec(memory_space=pltpu.HBM)
IN_SMEM = pl.BlockSpec(memory_space=pltpu.SMEM)


def hbm(array):
    return pltpu.with_memory_space_constraint(array, pltpu.HBM)


def vmem(array):
    return pltpu.with_memory_space_constraint(array, pltpu.VMEM)


def run_copies(copies):
    for copy in copies:
        copy.start()
    for copy in copies:
        copy.wait()


def pick_kernel(ids_ref, stored_ref, out_ref, held_ref, loaded, done):
    count, block_rows, features = out_ref.shape
    first = stored_ref.shape[1] - features
    loads = [
        pltpu.make_async_copy(
            stored_ref.at[
                pl.ds(pl.multiple_of(ids_ref[i] * block_rows, block_rows), block_rows),
                pl.ds(first, features),
            ],
            held_ref.at[i],
            loaded.at[i],
        )
        for i in range(count)
    ]
    stores = [
        pltpu.make_async_copy(held_ref.at[i], out_ref.at[i], done.at[i]) for i in range(count)
    ]
    for load in loads[:WINDOW]:
        load.start()
    for i in range(count):
        loads[i].wait()
        stores[i].start()
        if i + WINDOW < count:
            loads[i + WINDOW].start()
    for store in stores:
        store.wait()


def pick_blocks(ids, passage_emb, block_rows, first):
    count, features = ids.shape[0], passage_emb.shape[1] - first
    return pl.pallas_call(
        pick_kernel,
        out_shape=pltpu.HBM((count, block_rows, features), passage_emb.dtype),
        in_specs=[IN_SMEM, IN_HBM],
        out_specs=IN_HBM,
        scratch_shapes=[
            pltpu.VMEM((count, block_rows, features), passage_emb.dtype),
            pltpu.SemaphoreType.DMA((count,)),
            pltpu.SemaphoreType.DMA((count,)),
        ],
        compiler_params=pltpu.CompilerParams(vmem_limit_bytes=VMEM_LIMIT),
        cost_estimate=pl.CostEstimate(
            flops=0, bytes_accessed=4 * count * block_rows * features, transcendentals=0
        ),
        name="pick_blocks",
    )(ids, hbm(passage_emb))


def pick_pairs_kernel(ids_ref, stored_ref, *refs):
    *far_refs, out_ref, done = refs
    count, _, block_rows, features = out_ref.shape
    copies = []

    def add(source, item, which, first, width):
        rows = pl.ds(pl.multiple_of(ids_ref[item, which] * block_rows, block_rows), block_rows)
        copies.append(
            pltpu.make_async_copy(
                source.at[rows, pl.ds(0, width)],
                out_ref.at[item, which, :, pl.ds(first, width)],
                done.at[len(copies)],
            )
        )

    for item in range(count):
        add(stored_ref, item, 0, 0, features)
        first = 0
        for far_ref in far_refs:
            add(far_ref, item, 1, first, far_ref.shape[1])
            first += far_ref.shape[1]
    run_copies(copies)


def pick_pairs(ids, passage_emb, far_parts, block_rows):
    count = ids.shape[0]
    features = sum(part.shape[1] for part in far_parts)
    return pl.pallas_call(
        pick_pairs_kernel,
        out_shape=pltpu.VMEM((count, 2, block_rows, features), passage_emb.dtype),
        in_specs=[IN_SMEM] + [IN_HBM] * (1 + len(far_parts)),
        out_specs=IN_VMEM,
        scratch_shapes=[pltpu.SemaphoreType.DMA((count * (1 + len(far_parts)),))],
        compiler_params=pltpu.CompilerParams(vmem_limit_bytes=VMEM_LIMIT),
        cost_estimate=pl.CostEstimate(flops=10**12, bytes_accessed=10**9, transcendentals=0),
        name="pick_pairs",
    )(ids, hbm(passage_emb), *[hbm(part) for part in far_parts])


def score_kernel(
    near_slots_ref, slots_ref, query_ref, positive_ref, near_ref, fetched_ref, *refs
):
    score_ref, listed_ref, held_positive_ref, near_done, done = refs
    query_blocks, list_len = slots_ref.shape
    block_rows, near_features = near_ref.shape[1:]
    held_positive_ref[...] = positive_ref[...]
    copies = []
    for b in range(query_blocks):
        for j in range(list_len):
            i = b * list_len + j
            for source_ref, table_ref, first, arrived in (
                (near_ref, near_slots_ref, 0, near_done),
                (fetched_ref, slots_ref, near_features, done),
            ):
                copies.append(
                    pltpu.make_async_copy(
                        source_ref.at[table_ref[b, j]],
                        listed_ref.at[i, :, pl.ds(first, source_ref.shape[2])],
                        arrived.at[i],
                    )
                )
    for copy in copies:
        copy.start()
    for b in range(query_blocks):
        for copy in copies[2 * b * list_len : 2 * (b + 1) * list_len]:
            copy.wait()
        listed = listed_ref[b * list_len : (b + 1) * list_len]
        score_ref[b] = lax.dot_general(
            query_ref[b * block_rows : (b + 1) * block_rows, :],
            listed.reshape(list_len * block_rows, listed.shape[2]),
            (((1,), (1,)), ((), ())),
            preferred_element_type=jnp.float32,
        )


def partial_scores(near_slots, slots, query_emb, positive, near, fetched):
    query_blocks, list_len = slots.shape
    block_rows = fetched.shape[1]
    features = query_emb.shape[1]
    columns = list_len * block_rows
    listed_count = query_blocks * list_len
    return pl.pallas_call(
        score_kernel,
        out_shape=(
            pltpu.VMEM((query_blocks, block_rows, columns), jnp.float32),
            pltpu.VMEM((listed_count, block_rows, features), fetched.dtype),
            pltpu.VMEM((query_blocks, 1, block_rows), jnp.int32),
        ),
        in_specs=[IN_SMEM] * 2 + [IN_VMEM] * 2 + [IN_HBM] * 2,
        out_specs=[IN_VMEM] * 3,
        scratch_shapes=[pltpu.SemaphoreType.DMA((listed_count,))] * 2,
        compiler_params=pltpu.CompilerParams(vmem_limit_bytes=VMEM_LIMIT),
        cost_estimate=pl.CostEstimate(
            flops=2 * query_blocks * block_rows * columns * features,
            bytes_accessed=2 * listed_count * block_rows * features + 2 * query_emb.size,
            transcendentals=0,
        ),
        name="partial_scores",
    )(
        near_slots,
        slots,
        query_emb,
        positive.reshape(query_blocks, 1, block_rows),
        hbm(near),
        hbm(fetched),
    )


def gradient_kernel(share_count, share_ref, *refs):
    score_refs = refs[:share_count]
    listed_ref, positive_ref, loss_ref, grad_ref = refs[share_count:]
    block = pl.program_id(0)
    block_rows, features = grad_ref.shape
    list_len = listed_ref.shape[0] // pl.num_programs(0)
    total = score_refs[0][block]
    for ref in score_refs[1:]:
        total = total + ref[block]
    scores = total * 50.0
    row_max = jnp.max(scores, axis=1, keepdims=True)
    log_total = row_max + jnp.log(jnp.sum(jnp.exp(scores - row_max), axis=1, keepdims=True))
    square = (block_rows, block_rows)
    positive = jnp.broadcast_to(positive_ref[block], square).T[:, :1]
    matched = lax.broadcasted_iota(jnp.int32, scores.shape, 1) == positive
    picked = jnp.sum(jnp.where(matched, scores, 0.0), axis=1, keepdims=True)
    losses = jnp.broadcast_to(log_total - picked, square).T[:1]
    held = loss_ref.shape[0]

    @pl.when(block // held == share_ref[0])
    def _():
        loss_ref[block % held] = losses

    weights = (jnp.exp(scores - log_total) - matched.astype(jnp.float32)).astype(jnp.bfloat16)
    tile = min(TILE, features)
    for f in range(0, features, tile):
        listed = listed_ref[pl.ds(block * list_len, list_len), :, f : f + tile]
        grad = jnp.dot(
            weights,
            listed.reshape(list_len * block_rows, tile),
            preferred_element_type=jnp.float32,
        )
        grad_ref[:, f : f + tile] = (grad * 50.0).astype(jnp.bfloat16)


def losses_and_gradients(share, share_blocks, scores, listed, positive):
    query_blocks, block_rows, columns = scores[0].shape
    features = listed.shape[2]
    rows = query_blocks * block_rows
    return pl.pallas_call(
        functools.partial(gradient_kernel, len(scores)),
        out_shape=(
            jax.ShapeDtypeStruct((share_blocks, 1, block_rows), jnp.float32),
            jax.ShapeDtypeStruct((rows, features), jnp.bfloat16),
        ),
        grid=(query_blocks,),
        in_specs=[IN_SMEM] + [IN_VMEM] * (len(scores) + 2),
        out_specs=[
            pl.BlockSpec((share_blocks, 1, block_rows), lambda b: (0, 0, 0)),
            pl.BlockSpec((block_rows, features), lambda b: (b, 0)),
        ],
        compiler_params=pltpu.CompilerParams(vmem_limit_bytes=VMEM_LIMIT),
        cost_estimate=pl.CostEstimate(
            flops=2 * rows * columns * features,
            bytes_accessed=2 * rows * features,
            transcendentals=2 * rows * columns,
        ),
        name="losses_and_gradients",
    )(share, *[vmem(score) for score in scores], vmem(listed), vmem(positive))


def shards(query_emb, passage_emb, cand_blocks, positive):
    dp_count = lax.axis_size("dp")
    fsdp_count = lax.axis_size("fsdp")
    query_blocks, list_len = cand_blocks.shape
    row_count, feature_count = query_emb.shape
    block_rows = row_count // query_blocks
    passage_blocks = passage_emb.shape[0] // block_rows
    half = dp_count // 2
    me = lax.axis_index("dp")
    me_in_half = me % half
    owners = cand_blocks // passage_blocks
    local_ids = cand_blocks % passage_blocks

    share = lax.axis_index("fsdp").astype(jnp.int32)
    to_other_half = [(d, (d + half) % dp_count) for d in range(dp_count)]
    first = LANES
    swapped = first + max(1, feature_count // LANES * 3 // 16) * LANES
    early_half = lax.ppermute(passage_emb[:, :first], "dp", to_other_half)

    owner_index = lax.broadcasted_iota(jnp.int32, (dp_count, query_blocks, list_len), 0)
    other_half = (owner_index + half) % dp_count == owners[None]
    both_ids = jnp.where(owner_index == owners[None], local_ids[None], 0) + jnp.where(
        other_half, SHIFT * local_ids[None], 0
    )
    both_tables = jnp.sum(both_ids, axis=(1, 2)).reshape(dp_count, 1)
    both_tables, share = lax.optimization_barrier((both_tables, share))
    requested = lax.all_to_all(both_tables, "dp", split_axis=0, concat_axis=0, tiled=True)
    requested = requested.reshape(dp_count)
    requested, early_half = lax.optimization_barrier((requested, early_half))
    late_half, requested = lax.optimization_barrier((passage_emb[:, first:swapped], requested))
    far_parts = [early_half, lax.ppermute(late_half, "dp", to_other_half)]
    picked = pick_blocks(requested % SHIFT, passage_emb, block_rows, swapped)
    fetched = lax.all_to_all(picked, "dp", split_axis=0, concat_axis=0, tiled=True)

    steps = jnp.arange(half, dtype=jnp.int32)
    readers = me - me_in_half + (me_in_half + steps) % half
    relayed = requested[readers]
    relayed = jnp.stack([relayed % SHIFT, relayed // SHIFT], axis=1)
    pairs = pick_pairs(relayed, passage_emb, far_parts, block_rows)
    near = jnp.concatenate(
        [pairs[0]]
        + [
            lax.ppermute(
                pairs[k],
                "dp",
                [(d, d - d % half + (d % half + k) % half) for d in range(dp_count)],
            )
            for k in range(1, half)
        ],
        axis=0,
    )
    near_slots = 2 * ((me_in_half - owners) % half) + (owners // half != me // half)
    near_slots = near_slots.astype(jnp.int32)

    mine, listed, positive = partial_scores(
        near_slots, owners, query_emb, positive, near, fetched
    )
    scores = [mine] + [
        lax.ppermute(mine, "fsdp", [(i, (i + k) % fsdp_count) for i in range(fsdp_count)])
        for k in range(1, fsdp_count)
    ]
    share_rows = row_count // fsdp_count
    if share_rows % block_rows == 0:
        losses, query_grad = losses_and_gradients(
            share.reshape(1), share_rows // block_rows, scores, listed, positive
        )
        return losses.reshape(share_rows), query_grad
    whole = jnp.zeros((1,), jnp.int32)
    losses, query_grad = losses_and_gradients(whole, query_blocks, scores, listed, positive)
    losses = lax.dynamic_slice_in_dim(losses.reshape(row_count), share * share_rows, share_rows)
    return losses, query_grad


def solution(mesh):
    return jax.shard_map(
        shards,
        mesh=mesh,
        in_specs=(P("dp", "fsdp"), P("dp", "fsdp"), P("dp", None), P("dp")),
        out_specs=(P(("dp", "fsdp")), P("dp", "fsdp")),
        check_vma=False,
    )
```

time: 268 us -> 214 us (0.80)
  waiting for transfers between devices: 198 us -> 123 us
  starting transfers between devices: 6.75 us -> 58 us
  Pallas kernels: 0 us -> 18.4 us
  between operations: 14.1 us -> 0.76 us
  matrix products: 13.3 us -> 0 us
  blocking collectives: 12.8 us -> 0 us
  local copies, waits for them, and re-layouts: 16.3 us -> 10.4 us
  other arithmetic: 5.09 us -> 1.23 us
    all_to_all x1 -> x2, waiting for transfers between devices: 184 us -> 17.5 us  [the longest x1 13.1 us: shards(): lax.all_to_all(picked, 'dp', split_axis=0, concat_axis=0, tiled=True)]
    ppermute x0 -> x10, waiting for transfers between devices: none -> 106 us  [the longest x7 81.9 us: shards(): lax.ppermute(pairs[k], 'dp', [(d, d - d % half + (d % half + k) % half) f...]
    ppermute x0 -> x10, starting transfers between devices: none -> 47.8 us  [the longest x7 41.1 us: shards(): lax.ppermute(pairs[k], 'dp', [(d, d - d % half + (d % half + k) % half) f...]
    pallas_call x0 -> x4, Pallas kernels: none -> 18.4 us  [the longest x1 6.02 us: pick_blocks(): pl.pallas_call(pick_kernel, out_shape=pltpu.HBM((count, block_rows, featu...]
    gather x2 -> x1, local copies, waits for them, and re-layouts: 15.1 us -> 0.64 us  [shards(): relayed = requested[readers]]
    reduce_scatter x1 -> x0, waiting for transfers between devices: 13.6 us -> none  [shards(): lax.psum_scatter(partial_value, 'fsdp', scatter_dimension=0, tiled=True)]
    dot_general x2 -> x0, matrix products: 13.3 us -> none  [the longest x1 7.29 us: shards(): jnp.einsum('qnd,qcd->qnc', query_rows, candidates, preferred_element_type...]
    all_to_all x1 -> x0, blocking collectives: 10.6 us -> none  [shards(): lax.all_to_all(id_table, 'dp', split_axis=0, concat_axis=0, tiled=True)]
  transfers between devices with their start and end apart: 2 -> 12, of which waited for: 2 -> 7; matrix products, arithmetic and copies ran while one was open for 0% -> 5% of each run, Pallas kernels for 0% -> 4%
where the time goes in v2:
time: 214 us; the launch traced here: 212 us
  waiting for transfers between devices  123 us (57%)
  starting transfers between devices  58 us (27%)
  Pallas kernels  18.4 us (9%)
  local copies, waits for them, and re-layouts  10.4 us (5%)
    ppermute x7, waiting for transfers between devices, shards(): lax.ppermute(pairs[k], 'dp', [(d, d - d % half + (d % half + k) % half) f...  81.9 us
    ppermute x7, starting transfers between devices, shards(): lax.ppermute(pairs[k], 'dp', [(d, d - d % half + (d % half + k) % half) f...  41.1 us
    ppermute x1, waiting for transfers between devices, shards(): far_parts = [early_half, lax.ppermute(late_half, 'dp', to_other_half)]  21.7 us
    all_to_all x1, waiting for transfers between devices, shards(): lax.all_to_all(picked, 'dp', split_axis=0, concat_axis=0, tiled=True)  13.1 us
    pallas_call x1, Pallas kernels, pick_blocks(): pl.pallas_call(pick_kernel, out_shape=pltpu.HBM((count, block_rows, featu...  6.02 us
    unnamed x19, local copies, waits for them, and re-layouts  5.94 us
    pallas_call x1, Pallas kernels, partial_scores(): pl.pallas_call(score_kernel, out_shape=(pltpu.VMEM((query_blocks, block_r...  5.77 us
    all_to_all x1, starting transfers between devices, shards(): lax.all_to_all(picked, 'dp', split_axis=0, concat_axis=0, tiled=True)  5.61 us
  transfers between devices with their start and end apart: 12, of which 7 were waited for; matrix products, arithmetic and copies ran while one was open for 5% of the time, Pallas kernels for 4%

profile of v2, /device:TPU:11, one launch (start us, length us, event | category | flops | bytes accessed | tf_op | source)
XLA Modules:
  0.0 212.1 jit_solution(5385653017916859972)
XLA Ops:
  0.6 1.0 slice.31
  1.6 2.4 %collective-permute-start = (bf16[1024,128]{1,0:T(8,128)(2,1)S(1)}, bf16[1024,128]{1,0:T(8,128)(2,1)S(1)}, u32[]{:S(2)}, u32[]{:S(2)}) collective-permute-start(bf16[1024,128]{1,0:T(8,128)(2,1)S(1)} %slice.31), channel_id=1, source_target_pairs={{0,16},{2,18},{4,20},{6,22},{8,24},{10,26},{12,28},{14,30},{16,0},... | collective-permute-start | bytes 786440 | tf_op jit(solution)/shard_map/ppermute | solution.py:269
  4.0 0.7 fusion.3
  4.7 0.0 copy-start.1
  4.7 0.1 add_reduce_fusion
  4.8 0.7 copy.18
  5.5 4.6 %all-to-all-start = ((s32[16,1,1]{2,1,0:T(1,128)}), s32[16,1,1]{2,1,0:T(1,128)S(1)}, u32[]{:S(2)}, u32[]{:S(2)}) async-start(s32[16,1,1]{2,1,0:T(1,128)} %copy.18), calls=%async_computation | async-start | bytes 16384 | tf_op jit(solution)/shard_map/all_to_all | solution.py:278
  10.1 1.2 slice.30
  11.3 4.4 %all-to-all-done = s32[16,1,1]{2,1,0:T(1,128)S(1)} async-done(((s32[16,1,1]{2,1,0:T(1,128)}), s32[16,1,1]{2,1,0:T(1,128)S(1)}, u32[]{:S(2)}, u32[]{:S(2)}) %all-to-all-start) | async-done | bytes 96 | tf_op jit(solution)/shard_map/all_to_all | solution.py:278
  15.7 0.4 reduce
  16.1 0.0 collective-permute-done.refs_0_
  16.1 0.0 copy-start.5
  16.1 3.7 %collective-permute-start.1 = (bf16[1024,384]{1,0:T(8,128)(2,1)S(1)}, bf16[1024,384]{1,0:T(8,128)(2,1)S(1)}, u32[]{:S(2)}, u32[]{:S(2)}) collective-permute-start(bf16[1024,384]{1,0:T(8,128)(2,1)S(1)} %slice.30), channel_id=1, source_target_pairs={{0,16},{2,18},{4,20},{6,22},{8,24},{10,26},{12,28},{14,30},{16,0},... | collective-permute-start | bytes 2359304 | tf_op jit(solution)/shard_map/ppermute | solution.py:282
  19.8 0.6 gather_fusion
  20.5 0.1 copy.19.ids_ref
  20.6 6.0 %pick_blocks.1 = bf16[16,128,1536]{2,1,0:T(8,128)(2,1)} custom-call(s32[16]{0:T(128)S(1)} %and_select_fusion.ids_ref, bf16[1024,2048]{1,0:T(8,128)(2,1)} %stored_ref.3), custom_call_target="tpu_custom_call" | custom-call | bytes 12582912 | tf_op jit(solution)/shard_map/pick_blocks/pallas_call | solution.py:65
  26.6 0.0 copy-done.1
  26.7 0.0 copy-done.5
  26.7 5.6 %all-to-all-start.1 = ((bf16[16,128,1536]{2,1,0:T(8,128)(2,1)}), bf16[16,128,1536]{2,1,0:T(8,128)(2,1)}, u32[]{:S(2)}, u32[]{:S(2)}) async-start(bf16[16,128,1536]{2,1,0:T(8,128)(2,1)} %pick_blocks.1), calls=%async_computation.1 | async-start | bytes 12582912 | tf_op jit(solution)/shard_map/all_to_all | solution.py:284
  32.3 21.7 %collective-permute-done.1.refs_1_ = bf16[1024,384]{1,0:T(8,128)(2,1)S(1)} collective-permute-done((bf16[1024,384]{1,0:T(8,128)(2,1)S(1)}, bf16[1024,384]{1,0:T(8,128)(2,1)S(1)}, u32[]{:S(2)}, u32[]{:S(2)}) %collective-permute-start.1) | collective-permute-done | bytes 786464 | tf_op jit(solution)/shard_map/ppermute | solution.py:282
  53.9 0.0 copy-start.4
  53.9 0.9 copy-done.4
  54.8 2.4 %pick_pairs.1 = bf16[8,2,128,512]{3,2,1,0:T(8,128)(2,1)S(1)} custom-call(s32[8,2]{1,0:T(8,128)S(1)} %copy.19.ids_ref, bf16[1024,2048]{1,0:T(8,128)(2,1)} %stored_ref.3, bf16[1024,128]{1,0:T(8,128)(2,1)} %copy-done.5, bf16[1024,384]{1,0:T(8,128)(2,1)} %copy-done.4), custom_call_target="tpu_custom_call" | custom-call | flops 999999995904 | bytes 1000000000 | tf_op jit(solution)/shard_map/pick_pairs/pallas_call | solution.py:110
  57.2 0.1 slice_bitcast_fusion
  57.4 36.0 %collective-permute-start.2 = (bf16[2,128,512]{2,1,0:T(8,128)(2,1)S(1)}, bf16[2,128,512]{2,1,0:T(8,128)(2,1)S(1)}, u32[]{:S(2)}, u32[]{:S(2)}) collective-permute-start(bf16[2,128,512]{2,1,0:T(8,128)(2,1)S(1)} %get-tuple-element.34), channel_id=1, source_target_pairs={{0,2},{2,4},{4,6},{6,8},{8,10},{10,12},{12,14},{14,0},{16,18},{18,... | collective-permute-start | bytes 786440 | tf_op jit(solution)/shard_map/ppermute | solution.py:294
  93.4 2.7 %collective-permute-start.4 = (bf16[2,128,512]{2,1,0:T(8,128)(2,1)S(1)}, bf16[2,128,512]{2,1,0:T(8,128)(2,1)S(1)}, u32[]{:S(2)}, u32[]{:S(2)}) collective-permute-start(bf16[2,128,512]{2,1,0:T(8,128)(2,1)S(1)} %get-tuple-element.32), channel_id=1, source_target_pairs={{0,6},{2,8},{4,10},{6,12},{8,14},{10,0},{12,2},{14,4},{16,22},{18,... | collective-permute-start | bytes 786440 | tf_op jit(solution)/shard_map/ppermute | solution.py:294
  96.1 0.0 copy-start
  96.1 0.0 copy-start.2
  96.1 0.0 copy-start.3
  96.1 0.0 collective-permute-start.3
  96.1 0.7 fusion
  96.8 1.2 collective-permute-start.8
  98.0 1.1 collective-permute-start.7
  99.2 32.1 %collective-permute-done.2 = bf16[2,128,512]{2,1,0:T(8,128)(2,1)S(1)} collective-permute-done((bf16[2,128,512]{2,1,0:T(8,128)(2,1)S(1)}, bf16[2,128,512]{2,1,0:T(8,128)(2,1)S(1)}, u32[]{:S(2)}, u32[]{:S(2)}) %collective-permute-start.2) | collective-permute-done | bytes 262176 | tf_op jit(solution)/shard_map/ppermute | solution.py:294
  131.3 0.0 collective-permute-start.5
  131.3 0.7 constant_dynamic-update-slice_fusion.6
  132.0 37.0 %collective-permute-done.3 = bf16[2,128,512]{2,1,0:T(8,128)(2,1)S(1)} collective-permute-done((bf16[2,128,512]{2,1,0:T(8,128)(2,1)S(1)}, bf16[2,128,512]{2,1,0:T(8,128)(2,1)S(1)}, u32[]{:S(2)}, u32[]{:S(2)}) %collective-permute-start.3) | collective-permute-done | bytes 262176 | tf_op jit(solution)/shard_map/ppermute | solution.py:294
  169.0 0.0 collective-permute-start.6
  169.0 0.7 constant_dynamic-update-slice_fusion.5
  169.7 0.0 collective-permute-done.4
  169.7 0.7 constant_dynamic-update-slice_fusion.4
  170.4 0.0 collective-permute-done.5
  170.4 0.7 constant_dynamic-update-slice_fusion.3
  171.2 12.8 %collective-permute-done.6 = bf16[2,128,512]{2,1,0:T(8,128)(2,1)S(1)} collective-permute-done((bf16[2,128,512]{2,1,0:T(8,128)(2,1)S(1)}, bf16[2,128,512]{2,1,0:T(8,128)(2,1)S(1)}, u32[]{:S(2)}, u32[]{:S(2)}) %collective-permute-start.6) | collective-permute-done | bytes 262176 | tf_op jit(solution)/shard_map/ppermute | solution.py:294
  184.0 0.7 constant_dynamic-update-slice_fusion.2
  184.7 0.0 collective-permute-done.7
  184.7 0.7 constant_dynamic-update-slice_fusion.1
  185.4 0.0 collective-permute-done.8
  185.4 0.7 constant_dynamic-update-slice_fusion.near_ref
  186.1 13.1 %all-to-all-done.1.fetched_ref = bf16[16,128,1536]{2,1,0:T(8,128)(2,1)} async-done(((bf16[16,128,1536]{2,1,0:T(8,128)(2,1)}), bf16[16,128,1536]{2,1,0:T(8,128)(2,1)}, u32[]{:S(2)}, u32[]{:S(2)}) %all-to-all-start.1) | async-done | bytes 6291488 | tf_op jit(solution)/shard_map/all_to_all | solution.py:284
  199.3 0.0 copy-done
  199.3 0.0 copy-done.2
  199.3 0.0 copy-done.3
  199.3 5.8 %partial_scores.1 = (f32[4,128,512]{2,1,0:T(8,128)S(1)}, bf16[16,128,2048]{2,1,0:T(8,128)(2,1)S(1)}, s32[4,1,128]{2,1,0:T(1,128)S(1)}) custom-call(s32[4,4]{1,0:T(4,128)S(1)} %get-tuple-element.24.near_slots_ref, s32[4,4]{1,0:T(4,128)S(1)} %copy-done.2, bf16[512,2048]{1,0:T(8,128)(2,1)S(1)} %copy-done, s32[4,1,128]{2,1,0:T(1,128)S(1)} %bitcast.40, ...), custom_call_target="tpu_custom_call" | custom-call | flops 1073741824 | bytes 10485760 | tf_op jit(solution)/shard_map/partial_scores/pallas_call | solution.py:164
  205.0 0.6 collective-permute-start.9
  205.7 2.3 %collective-permute-done.9.refs_1_ = f32[4,128,512]{2,1,0:T(8,128)S(1)} collective-permute-done((f32[4,128,512]{2,1,0:T(8,128)S(1)}, f32[4,128,512]{2,1,0:T(8,128)S(1)}, u32[]{:S(2)}, u32[]{:S(2)}) %collective-permute-start.9) | collective-permute-done | bytes 1048608 | tf_op jit(solution)/shard_map/ppermute | solution.py:310
  207.9 4.2 %losses_and_gradients.1 = (f32[2,1,128]{2,1,0:T(1,128)}, bf16[512,2048]{1,0:T(8,128)(2,1)}) custom-call(s32[1]{0:T(128)} %bitcast.1.share_ref, f32[4,128,512]{2,1,0:T(8,128)S(1)} %get-tuple-element.19.refs_0_, f32[4,128,512]{2,1,0:T(8,128)S(1)} %collective-permute-done.9.refs_1_, bf16[16,128,2048]{2,1,0:T(8,128)(2,1)S(1)} %get-tuple-element.20.refs_2_, ...), custom_call_target="tpu_custom_call" | custom-call | flops 1073741824 | bytes 2097152 | tf_op jit(solution)/shard_map/losses_and_gradients/pallas_call | solution.py:230
  (7 shorter events, 0.1 us)
Async XLA Ops:
  1.6 14.5 %collective-permute-start = (bf16[1024,128]{1,0:T(8,128)(2,1)S(1)}, bf16[1024,128]{1,0:T(8,128)(2,1)S(1)}, u32[]{:S(2)}, u32[]{:S(2)}) collective-permute-start(bf16[1024,128]{1,0:T(8,128)(2,1)S(1)} %slice.31), channel_id=1, source_target_pairs={{0,16},{2,18},{4,20},{6,22},{8,24},{10,26},{12,28},{14,30},{16,0},... | collective-permute-start | bytes 786440 | tf_op jit(solution)/shard_map/ppermute | solution.py:269
  4.7 22.0 %copy-start.1 = (s32[4,4]{1,0:T(4,128)}, s32[4,4]{1,0:T(4,128)S(1)}, u32[]{:S(2)}) copy-start(s32[4,4]{1,0:T(4,128)S(1)} %get-tuple-element.25.slots_ref) | copy-start | bytes 196
  5.5 10.2 %all-to-all-start = ((s32[16,1,1]{2,1,0:T(1,128)}), s32[16,1,1]{2,1,0:T(1,128)S(1)}, u32[]{:S(2)}, u32[]{:S(2)}) async-start(s32[16,1,1]{2,1,0:T(1,128)} %copy.18), calls=%async_computation | async-start | bytes 16384 | tf_op jit(solution)/shard_map/all_to_all | solution.py:278
  16.1 10.6 %copy-start.5 = (bf16[1024,128]{1,0:T(8,128)(2,1)}, bf16[1024,128]{1,0:T(8,128)(2,1)S(1)}, u32[]{:S(2)}) copy-start(bf16[1024,128]{1,0:T(8,128)(2,1)S(1)} %collective-permute-done.refs_0_) | copy-start | bytes 786436
  16.1 37.8 %collective-permute-start.1 = (bf16[1024,384]{1,0:T(8,128)(2,1)S(1)}, bf16[1024,384]{1,0:T(8,128)(2,1)S(1)}, u32[]{:S(2)}, u32[]{:S(2)}) collective-permute-start(bf16[1024,384]{1,0:T(8,128)(2,1)S(1)} %slice.30), channel_id=1, source_target_pairs={{0,16},{2,18},{4,20},{6,22},{8,24},{10,26},{12,28},{14,30},{16,0},... | collective-permute-start | bytes 2359304 | tf_op jit(solution)/shard_map/ppermute | solution.py:282
  26.7 172.6 %all-to-all-start.1 = ((bf16[16,128,1536]{2,1,0:T(8,128)(2,1)}), bf16[16,128,1536]{2,1,0:T(8,128)(2,1)}, u32[]{:S(2)}, u32[]{:S(2)}) async-start(bf16[16,128,1536]{2,1,0:T(8,128)(2,1)} %pick_blocks.1), calls=%async_computation.1 | async-start | bytes 12582912 | tf_op jit(solution)/shard_map/all_to_all | solution.py:284
  53.9 0.9 copy-start.4
  57.4 73.9 %collective-permute-start.2 = (bf16[2,128,512]{2,1,0:T(8,128)(2,1)S(1)}, bf16[2,128,512]{2,1,0:T(8,128)(2,1)S(1)}, u32[]{:S(2)}, u32[]{:S(2)}) collective-permute-start(bf16[2,128,512]{2,1,0:T(8,128)(2,1)S(1)} %get-tuple-element.34), channel_id=1, source_target_pairs={{0,2},{2,4},{4,6},{6,8},{8,10},{10,12},{12,14},{14,0},{16,18},{18,... | collective-permute-start | bytes 786440 | tf_op jit(solution)/shard_map/ppermute | solution.py:294
  93.4 76.4 %collective-permute-start.4 = (bf16[2,128,512]{2,1,0:T(8,128)(2,1)S(1)}, bf16[2,128,512]{2,1,0:T(8,128)(2,1)S(1)}, u32[]{:S(2)}, u32[]{:S(2)}) collective-permute-start(bf16[2,128,512]{2,1,0:T(8,128)(2,1)S(1)} %get-tuple-element.32), channel_id=1, source_target_pairs={{0,6},{2,8},{4,10},{6,12},{8,14},{10,0},{12,2},{14,4},{16,22},{18,... | collective-permute-start | bytes 786440 | tf_op jit(solution)/shard_map/ppermute | solution.py:294
  96.1 103.2 %copy-start = (bf16[512,2048]{1,0:T(8,128)(2,1)S(1)}, bf16[512,2048]{1,0:T(8,128)(2,1)}, u32[]{:S(2)}) copy-start(bf16[512,2048]{1,0:T(8,128)(2,1)} %query_ref.1) | copy-start | bytes 6291460
  96.1 103.2 %copy-start.2 = (s32[4,4]{1,0:T(4,128)S(1)}, s32[4,4]{1,0:T(4,128)}, u32[]{:S(2)}) copy-start(s32[4,4]{1,0:T(4,128)} %copy-done.1) | copy-start | bytes 196
  96.1 103.2 %copy-start.3 = (s32[512]{0:T(512)S(1)}, s32[512]{0:T(512)}, u32[]{:S(2)}) copy-start(s32[512]{0:T(512)} %param.7) | copy-start | bytes 6148
  96.1 72.9 %collective-permute-start.3 = (bf16[2,128,512]{2,1,0:T(8,128)(2,1)S(1)}, bf16[2,128,512]{2,1,0:T(8,128)(2,1)S(1)}, u32[]{:S(2)}, u32[]{:S(2)}) collective-permute-start(bf16[2,128,512]{2,1,0:T(8,128)(2,1)S(1)} %get-tuple-element.33), channel_id=1, source_target_pairs={{0,4},{2,6},{4,8},{6,10},{8,12},{10,14},{12,0},{14,2},{16,20},{18,... | collective-permute-start | bytes 786440 | tf_op jit(solution)/shard_map/ppermute | solution.py:294
  96.8 88.6 %collective-permute-start.8 = (bf16[2,128,512]{2,1,0:T(8,128)(2,1)S(1)}, bf16[2,128,512]{2,1,0:T(8,128)(2,1)S(1)}, u32[]{:S(2)}, u32[]{:S(2)}) collective-permute-start(bf16[2,128,512]{2,1,0:T(8,128)(2,1)S(1)} %get-tuple-element.28), channel_id=1, source_target_pairs={{0,14},{2,0},{4,2},{6,4},{8,6},{10,8},{12,10},{14,12},{16,30},{18,... | collective-permute-start | bytes 786440 | tf_op jit(solution)/shard_map/ppermute | solution.py:294
  98.0 86.7 %collective-permute-start.7 = (bf16[2,128,512]{2,1,0:T(8,128)(2,1)S(1)}, bf16[2,128,512]{2,1,0:T(8,128)(2,1)S(1)}, u32[]{:S(2)}, u32[]{:S(2)}) collective-permute-start(bf16[2,128,512]{2,1,0:T(8,128)(2,1)S(1)} %get-tuple-element.29), channel_id=1, source_target_pairs={{0,12},{2,14},{4,0},{6,2},{8,4},{10,6},{12,8},{14,10},{16,28},{18,... | collective-permute-start | bytes 786440 | tf_op jit(solution)/shard_map/ppermute | solution.py:294
  131.3 39.2 %collective-permute-start.5 = (bf16[2,128,512]{2,1,0:T(8,128)(2,1)S(1)}, bf16[2,128,512]{2,1,0:T(8,128)(2,1)S(1)}, u32[]{:S(2)}, u32[]{:S(2)}) collective-permute-start(bf16[2,128,512]{2,1,0:T(8,128)(2,1)S(1)} %get-tuple-element.31), channel_id=1, source_target_pairs={{0,8},{2,10},{4,12},{6,14},{8,0},{10,2},{12,4},{14,6},{16,24},{18,... | collective-permute-start | bytes 786440 | tf_op jit(solution)/shard_map/ppermute | solution.py:294
  169.0 15.0 %collective-permute-start.6 = (bf16[2,128,512]{2,1,0:T(8,128)(2,1)S(1)}, bf16[2,128,512]{2,1,0:T(8,128)(2,1)S(1)}, u32[]{:S(2)}, u32[]{:S(2)}) collective-permute-start(bf16[2,128,512]{2,1,0:T(8,128)(2,1)S(1)} %get-tuple-element.30), channel_id=1, source_target_pairs={{0,10},{2,12},{4,14},{6,0},{8,2},{10,4},{12,6},{14,8},{16,26},{18,... | collective-permute-start | bytes 786440 | tf_op jit(solution)/shard_map/ppermute | solution.py:294
  205.0 2.9 %collective-permute-start.9 = (f32[4,128,512]{2,1,0:T(8,128)S(1)}, f32[4,128,512]{2,1,0:T(8,128)S(1)}, u32[]{:S(2)}, u32[]{:S(2)}) collective-permute-start(f32[4,128,512]{2,1,0:T(8,128)S(1)} %get-tuple-element.19.refs_0_), channel_id=1, source_target_pairs={{0,1},{1,0},{2,3},{3,2},{4,5},{5,4},{6,7},{7,6},{8,9},{9,8},{10,11... | collective-permute-start | bytes 3145736 | tf_op jit(solution)/shard_map/ppermute | solution.py:310

commit v3 on v2

--- a/solution.py
+++ b/solution.py
@@ -119,43 +119,95 @@
     )(ids, hbm(passage_emb), *[hbm(part) for part in far_parts])
 
 
+def block_copies(table_ref, block, source_ref, listed_ref, first, done):
+    list_len = table_ref.shape[1]
+    features = source_ref.shape[2]
+    return [
+        pltpu.make_async_copy(
+            source_ref.at[table_ref[block, j]],
+            listed_ref.at[block * list_len + j, :, pl.ds(first, features)],
+            done.at[block * list_len + j],
+        )
+        for j in range(list_len)
+    ]
+
+
+def block_scores(query_ref, listed_ref, block, list_len, first, features):
+    block_rows = listed_ref.shape[1]
+    listed = listed_ref[block * list_len : (block + 1) * list_len, :, first : first + features]
+    return lax.dot_general(
+        query_ref[block * block_rows : (block + 1) * block_rows, first : first + features],
+        listed.reshape(list_len * block_rows, features),
+        (((1,), (1,)), ((), ())),
+        preferred_element_type=jnp.float32,
+    )
+
+
+def near_score_kernel(near_slots_ref, query_ref, near_ref, score_ref, listed_ref, done):
+    query_blocks, list_len = near_slots_ref.shape
+    copies = [
+        block_copies(near_slots_ref, b, near_ref, listed_ref, 0, done)
+        for b in range(query_blocks)
+    ]
+    for copy in sum(copies, []):
+        copy.start()
+    for b in range(query_blocks):
+        for copy in copies[b]:
+            copy.wait()
+        score_ref[b] = block_scores(query_ref, listed_ref, b, list_len, 0, near_ref.shape[2])
+
+
+def near_scores(near_slots, query_emb, near):
+    query_blocks, list_len = near_slots.shape
+    _, block_rows, features = near.shape
+    columns = list_len * block_rows
+    listed_count = query_blocks * list_len
+    return pl.pallas_call(
+        near_score_kernel,
+        out_shape=jax.ShapeDtypeStruct((query_blocks, block_rows, columns), jnp.float32),
+        in_specs=[IN_SMEM, IN_VMEM, IN_HBM],
+        out_specs=IN_VMEM,
+        scratch_shapes=[
+            pltpu.VMEM((listed_count, block_rows, features), near.dtype),
+            pltpu.SemaphoreType.DMA((listed_count,)),
+        ],
+        compiler_params=pltpu.CompilerParams(vmem_limit_bytes=VMEM_LIMIT),
+        cost_estimate=pl.CostEstimate(
+            flops=2 * query_blocks * block_rows * columns * features,
+            bytes_accessed=2 * listed_count * block_rows * features + 2 * query_emb.size,
+            transcendentals=0,
+        ),
+        name="near_scores",
+    )(near_slots, query_emb, hbm(near))
+
+
 def score_kernel(
-    near_slots_ref, slots_ref, query_ref, positive_ref, near_ref, fetched_ref, *refs
+    near_slots_ref, slots_ref, query_ref, positive_ref, before_ref, near_ref, fetched_ref, *refs
 ):
     score_ref, listed_ref, held_positive_ref, near_done, done = refs
     query_blocks, list_len = slots_ref.shape
-    block_rows, near_features = near_ref.shape[1:]
+    near_features, features = near_ref.shape[2], fetched_ref.shape[2]
+    blocks = range(query_blocks)
+    copies = [
+        block_copies(slots_ref, b, fetched_ref, listed_ref, near_features, done) for b in blocks
+    ]
+    near_copies = [
+        block_copies(near_slots_ref, b, near_ref, listed_ref, 0, near_done) for b in blocks
+    ]
+    for copy in sum(copies + near_copies, []):
+        copy.start()
     held_positive_ref[...] = positive_ref[...]
-    copies = []
-    for b in range(query_blocks):
-        for j in range(list_len):
-            i = b * list_len + j
-            for source_ref, table_ref, first, arrived in (
-                (near_ref, near_slots_ref, 0, near_done),
-                (fetched_ref, slots_ref, near_features, done),
-            ):
-                copies.append(
-                    pltpu.make_async_copy(
-                        source_ref.at[table_ref[b, j]],
-                        listed_ref.at[i, :, pl.ds(first, source_ref.shape[2])],
-                        arrived.at[i],
-                    )
-                )
-    for copy in copies:
-        copy.start()
-    for b in range(query_blocks):
-        for copy in copies[2 * b * list_len : 2 * (b + 1) * list_len]:
+    for b in blocks:
+        for copy in copies[b]:
             copy.wait()
-        listed = listed_ref[b * list_len : (b + 1) * list_len]
-        score_ref[b] = lax.dot_general(
-            query_ref[b * block_rows : (b + 1) * block_rows, :],
-            listed.reshape(list_len * block_rows, listed.shape[2]),
-            (((1,), (1,)), ((), ())),
-            preferred_element_type=jnp.float32,
-        )
-
-
-def partial_scores(near_slots, slots, query_emb, positive, near, fetched):
+        score_ref[b] = before_ref[b] + block_scores(
+            query_ref, listed_ref, b, list_len, near_features, features
+        )
+    for copy in sum(near_copies, []):
+        copy.wait()
+
+
+def partial_scores(near_slots, slots, query_emb, positive, before, near, fetched):
     query_blocks, list_len = slots.shape
     block_rows = fetched.shape[1]
     features = query_emb.shape[1]
@@ -168,12 +220,12 @@
             pltpu.VMEM((listed_count, block_rows, features), fetched.dtype),
             pltpu.VMEM((query_blocks, 1, block_rows), jnp.int32),
         ),
-        in_specs=[IN_SMEM] * 2 + [IN_VMEM] * 2 + [IN_HBM] * 2,
+        in_specs=[IN_SMEM] * 2 + [IN_VMEM] * 3 + [IN_HBM] * 2,
         out_specs=[IN_VMEM] * 3,
         scratch_shapes=[pltpu.SemaphoreType.DMA((listed_count,))] * 2,
         compiler_params=pltpu.CompilerParams(vmem_limit_bytes=VMEM_LIMIT),
         cost_estimate=pl.CostEstimate(
-            flops=2 * query_blocks * block_rows * columns * features,
+            flops=2 * query_blocks * block_rows * columns * fetched.shape[2],
             bytes_accessed=2 * listed_count * block_rows * features + 2 * query_emb.size,
             transcendentals=0,
         ),
@@ -183,6 +235,7 @@
         slots,
         query_emb,
         positive.reshape(query_blocks, 1, block_rows),
+        before,
         hbm(near),
         hbm(fetched),
     )
@@ -263,13 +316,14 @@
     local_ids = cand_blocks % passage_blocks
 
     share = lax.axis_index("fsdp").astype(jnp.int32)
-    to_other_half = [(d, (d + half) % dp_count) for d in range(dp_count)]
+    far = half + half // 2
+    to_other_half = [(d, d ^ far) for d in range(dp_count)]
     first = LANES
     swapped = first + max(1, feature_count // LANES * 3 // 16) * LANES
     early_half = lax.ppermute(passage_emb[:, :first], "dp", to_other_half)
 
     owner_index = lax.broadcasted_iota(jnp.int32, (dp_count, query_blocks, list_len), 0)
-    other_half = (owner_index + half) % dp_count == owners[None]
+    other_half = (owner_index ^ far) == owners[None]
     both_ids = jnp.where(owner_index == owners[None], local_ids[None], 0) + jnp.where(
         other_half, SHIFT * local_ids[None], 0
     )
@@ -280,8 +334,15 @@
     requested, early_half = lax.optimization_barrier((requested, early_half))
     late_half, requested = lax.optimization_barrier((passage_emb[:, first:swapped], requested))
     far_parts = [early_half, lax.ppermute(late_half, "dp", to_other_half)]
-    picked = pick_blocks(requested % SHIFT, passage_emb, block_rows, swapped)
-    fetched = lax.all_to_all(picked, "dp", split_axis=0, concat_axis=0, tiled=True)
+    quarter = dp_count // 4
+    order = [quarter * z + c for c in range(quarter) for z in (0, 3, 1, 2)]
+    slots = jnp.asarray([order.index(d) for d in range(dp_count)], jnp.int32)[owners]
+    picked = pick_blocks(
+        (requested % SHIFT)[jnp.asarray(order, jnp.int32)], passage_emb, block_rows, swapped
+    )
+    fetched = lax.all_to_all(
+        picked, "dp", split_axis=0, concat_axis=0, tiled=True, axis_index_groups=[order]
+    )
 
     steps = jnp.arange(half, dtype=jnp.int32)
     readers = me - me_in_half + (me_in_half + steps) % half
@@ -300,11 +361,13 @@
         ],
         axis=0,
     )
-    near_slots = 2 * ((me_in_half - owners) % half) + (owners // half != me // half)
+    is_far = (owners // half != me // half).astype(jnp.int32)
+    near_slots = 2 * ((me - (owners ^ (far * is_far))) % half) + is_far
     near_slots = near_slots.astype(jnp.int32)
 
+    before = near_scores(near_slots, query_emb, near)
     mine, listed, positive = partial_scores(
-        near_slots, owners, query_emb, positive, near, fetched
+        near_slots, slots, query_emb, positive, before, near, fetched
     )
     scores = [mine] + [
         lax.ppermute(mine, "fsdp", [(i, (i + k) % fsdp_count) for i in range(fsdp_count)])

time: 214 us -> 208 us (0.972)
  starting transfers between devices: 58 us -> 23 us
  waiting for transfers between devices: 123 us -> 150 us
  Pallas kernels: 18.4 us -> 20.8 us
    ppermute x7, starting transfers between devices: 41.1 us -> 4.94 us  [shards(): lax.ppermute(pairs[k], 'dp', [(d, d - d % half + (d % half + k) % half) f...]
    ppermute x7, waiting for transfers between devices: 81.9 us -> 108 us  [shards(): lax.ppermute(pairs[k], 'dp', [(d, d - d % half + (d % half + k) % half) f...]
    all_to_all x1, waiting for transfers between devices: 13.1 us -> 17.6 us  [shards(): lax.all_to_all(picked, 'dp', split_axis=0, concat_axis=0, tiled=True, axi...]
    ppermute x1, waiting for transfers between devices: 21.7 us -> 17.9 us  [shards(): far_parts = [early_half, lax.ppermute(late_half, 'dp', to_other_half)]]
    pallas_call x0 -> x1, Pallas kernels: none -> 3.05 us  [near_scores(): pl.pallas_call(near_score_kernel, out_shape=jax.ShapeDtypeStruct((query_b...]
    ppermute x1, starting transfers between devices: 3.71 us -> 1.26 us  [shards(): far_parts = [early_half, lax.ppermute(late_half, 'dp', to_other_half)]]
    unnamed x19 -> x25, local copies, waits for them, and re-layouts: 5.94 us -> 5.7 us
  transfers between devices with their start and end apart: 12 -> 12, of which waited for: 7 -> 8; matrix products, arithmetic and copies ran while one was open for 5% -> 4% of each run, Pallas kernels for 4% -> 6%
where the time goes in v3:
time: 208 us
  waiting for transfers between devices  150 us (72%)
  starting transfers between devices  23 us (11%)
  Pallas kernels  20.8 us (10%)
  local copies, waits for them, and re-layouts  12.3 us (6%)
    ppermute x7, waiting for transfers between devices, shards(): lax.ppermute(pairs[k], 'dp', [(d, d - d % half + (d % half + k) % half) f...  108 us
    ppermute x1, waiting for transfers between devices, shards(): far_parts = [early_half, lax.ppermute(late_half, 'dp', to_other_half)]  17.9 us
    all_to_all x1, waiting for transfers between devices, shards(): lax.all_to_all(picked, 'dp', split_axis=0, concat_axis=0, tiled=True, axi...  17.6 us
    all_to_all x1, starting transfers between devices, shards(): lax.all_to_all(picked, 'dp', split_axis=0, concat_axis=0, tiled=True, axi...  7.39 us
    pallas_call x1, Pallas kernels, pick_blocks(): pl.pallas_call(pick_kernel, out_shape=pltpu.HBM((count, block_rows, featu...  6.03 us
    unnamed x25, local copies, waits for them, and re-layouts  5.7 us
    all_to_all x1, starting transfers between devices, shards(): lax.all_to_all(both_tables, 'dp', split_axis=0, concat_axis=0, tiled=True)  5.62 us
    ppermute x7, starting transfers between devices, shards(): lax.ppermute(pairs[k], 'dp', [(d, d - d % half + (d % half + k) % half) f...  4.94 us
  transfers between devices with their start and end apart: 12, of which 8 were waited for; matrix products, arithmetic and copies ran while one was open for 4% of the time, Pallas kernels for 6%

profile of v3, /device:TPU:11, one launch (start us, length us, event | category | flops | bytes accessed | tf_op | source)
XLA Modules:
  0.0 207.8 jit_solution(14069263052291832379)
XLA Ops:
  0.6 0.0 copy-start.6
  0.6 1.0 slice.31
  1.6 1.4 collective-permute-start
  3.0 0.7 add_select_fusion
  3.7 0.1 add_reduce_fusion
  3.8 0.7 copy.20
  4.5 5.6 %all-to-all-start = ((s32[16,1,1]{2,1,0:T(1,128)}), s32[16,1,1]{2,1,0:T(1,128)S(1)}, u32[]{:S(2)}, u32[]{:S(2)}) async-start(s32[16,1,1]{2,1,0:T(1,128)} %copy.20), calls=%async_computation | async-start | bytes 16384 | tf_op jit(solution)/shard_map/all_to_all | solution.py:332
  10.1 1.2 slice.30
  11.3 4.1 %all-to-all-done = s32[16,1,1]{2,1,0:T(1,128)S(1)} async-done(((s32[16,1,1]{2,1,0:T(1,128)}), s32[16,1,1]{2,1,0:T(1,128)S(1)}, u32[]{:S(2)}, u32[]{:S(2)}) %all-to-all-start) | async-done | bytes 96 | tf_op jit(solution)/shard_map/all_to_all | solution.py:332
  15.4 0.4 reduce
  15.8 0.0 collective-permute-done.refs_0_
  15.8 0.0 copy-start.8
  15.8 1.3 collective-permute-start.1
  17.0 0.0 copy-done.6
  17.1 0.6 reshape.157
  17.7 0.6 gather_fusion.1
  18.4 0.1 copy.21.ids_ref
  18.4 0.7 gather_fusion.2
  19.1 6.0 %pick_blocks.1 = bf16[16,128,1536]{2,1,0:T(8,128)(2,1)} custom-call(s32[16]{0:T(128)S(1)} %gather_fusion.2, bf16[1024,2048]{1,0:T(8,128)(2,1)} %stored_ref.3), custom_call_target="tpu_custom_call" | custom-call | bytes 12582912 | tf_op jit(solution)/shard_map/pick_blocks/pallas_call | solution.py:65
  25.1 0.0 copy-done.8
  25.1 7.4 %all-to-all-start.1 = ((bf16[16,128,1536]{2,1,0:T(8,128)(2,1)}), bf16[16,128,1536]{2,1,0:T(8,128)(2,1)}, u32[]{:S(2)}, u32[]{:S(2)}) async-start(bf16[16,128,1536]{2,1,0:T(8,128)(2,1)} %pick_blocks.1), calls=%async_computation.1 | async-start | bytes 12582912 | tf_op jit(solution)/shard_map/all_to_all | solution.py:343
  32.5 17.9 %collective-permute-done.1.refs_1_ = bf16[1024,384]{1,0:T(8,128)(2,1)S(1)} collective-permute-done((bf16[1024,384]{1,0:T(8,128)(2,1)S(1)}, bf16[1024,384]{1,0:T(8,128)(2,1)S(1)}, u32[]{:S(2)}, u32[]{:S(2)}) %collective-permute-start.1) | collective-permute-done | bytes 786464 | tf_op jit(solution)/shard_map/ppermute | solution.py:336
  50.4 0.0 copy-start.7
  50.4 0.9 copy-done.7
  51.3 2.6 %pick_pairs.1 = bf16[8,2,128,512]{3,2,1,0:T(8,128)(2,1)S(1)} custom-call(s32[8,2]{1,0:T(8,128)S(1)} %copy.21.ids_ref, bf16[1024,2048]{1,0:T(8,128)(2,1)} %stored_ref.3, bf16[1024,128]{1,0:T(8,128)(2,1)} %copy-done.8, bf16[1024,384]{1,0:T(8,128)(2,1)} %copy-done.7), custom_call_target="tpu_custom_call" | custom-call | flops 999999995904 | bytes 1000000000 | tf_op jit(solution)/shard_map/pick_pairs/pallas_call | solution.py:110
  53.9 0.0 copy-start.1
  54.0 1.3 copy-done.1
  55.3 0.0 copy-start.5
  55.3 0.0 copy-start.3
  55.3 1.0 slice_bitcast_fusion
  56.3 1.0 collective-permute-start.2
  57.3 0.0 copy-done.5
  57.3 0.0 copy-done.3
  57.4 0.7 gather_fusion
  58.0 0.1 reshape.156.slots_ref
  58.1 0.0 collective-permute-start.4
  58.1 0.0 copy-start
  58.1 0.1 collective-permute-start.3
  58.2 1.1 fusion
  59.3 1.1 collective-permute-start.8
  60.4 2.4 %collective-permute-start.7 = (bf16[2,128,512]{2,1,0:T(8,128)(2,1)S(1)}, bf16[2,128,512]{2,1,0:T(8,128)(2,1)S(1)}, u32[]{:S(2)}, u32[]{:S(2)}) collective-permute-start(bf16[2,128,512]{2,1,0:T(8,128)(2,1)S(1)} %get-tuple-element.29), channel_id=1, source_target_pairs={{0,12},{2,14},{4,0},{6,2},{8,4},{10,6},{12,8},{14,10},{16,28},{18,... | collective-permute-start | bytes 786440 | tf_op jit(solution)/shard_map/ppermute | solution.py:355
  62.8 16.8 %collective-permute-done.2 = bf16[2,128,512]{2,1,0:T(8,128)(2,1)} collective-permute-done((bf16[2,128,512]{2,1,0:T(8,128)(2,1)}, bf16[2,128,512]{2,1,0:T(8,128)(2,1)}, u32[]{:S(2)}, u32[]{:S(2)}) %collective-permute-start.2) | collective-permute-done | bytes 262176 | tf_op jit(solution)/shard_map/ppermute | solution.py:355
  79.6 0.3 collective-permute-start.5
  79.9 1.0 constant_dynamic-update-slice_fusion.6
  80.9 78.8 %collective-permute-done.3 = bf16[2,128,512]{2,1,0:T(8,128)(2,1)S(1)} collective-permute-done((bf16[2,128,512]{2,1,0:T(8,128)(2,1)}, bf16[2,128,512]{2,1,0:T(8,128)(2,1)S(1)}, u32[]{:S(2)}, u32[]{:S(2)}) %collective-permute-start.3) | collective-permute-done | bytes 262176 | tf_op jit(solution)/shard_map/ppermute | solution.py:355
  159.7 0.0 collective-permute-start.6
  159.7 0.0 collective-permute-done.4
  159.7 0.8 collective-permute-done.5
  160.5 11.4 %collective-permute-done.6 = bf16[2,128,512]{2,1,0:T(8,128)(2,1)S(1)} collective-permute-done((bf16[2,128,512]{2,1,0:T(8,128)(2,1)S(1)}, bf16[2,128,512]{2,1,0:T(8,128)(2,1)S(1)}, u32[]{:S(2)}, u32[]{:S(2)}) %collective-permute-start.6) | collective-permute-done | bytes 262176 | tf_op jit(solution)/shard_map/ppermute | solution.py:355
  172.0 0.0 collective-permute-done.7
  172.0 0.0 collective-permute-done.8
  172.1 0.0 copy-start.4
  172.1 1.3 copy-done.4
  173.4 0.0 copy-done
  173.4 0.0 copy-start.2
  173.4 3.0 %near_scores.1.before_ref = f32[4,128,512]{2,1,0:T(8,128)S(1)} custom-call(s32[4,4]{1,0:T(4,128)S(1)} %fusion.5.near_slots_ref, bf16[512,2048]{1,0:T(8,128)(2,1)S(1)} %copy-done, bf16[16,128,512]{2,1,0:T(8,128)(2,1)} %copy-done.4), custom_call_target="tpu_custom_call" | custom-call | flops 268435456 | bytes 4194304 | tf_op jit(solution)/shard_map/near_scores/pallas_call | solution.py:165
  176.4 17.6 %all-to-all-done.1.fetched_ref = bf16[16,128,1536]{2,1,0:T(8,128)(2,1)} async-done(((bf16[16,128,1536]{2,1,0:T(8,128)(2,1)}), bf16[16,128,1536]{2,1,0:T(8,128)(2,1)}, u32[]{:S(2)}, u32[]{:S(2)}) %all-to-all-start.1) | async-done | bytes 6291488 | tf_op jit(solution)/shard_map/all_to_all | solution.py:343
  194.1 0.0 copy-done.2
  194.1 4.9 %partial_scores.1 = (f32[4,128,512]{2,1,0:T(8,128)S(1)}, bf16[16,128,2048]{2,1,0:T(8,128)(2,1)S(1)}, s32[4,1,128]{2,1,0:T(1,128)S(1)}) custom-call(s32[4,4]{1,0:T(4,128)S(1)} %fusion.5.near_slots_ref, s32[4,4]{1,0:T(4,128)S(1)} %reshape.156.slots_ref, bf16[512,2048]{1,0:T(8,128)(2,1)S(1)} %copy-done, s32[4,1,128]{2,1,0:T(1,128)S(1)} %bitcast.40, ...), custom_call_target="tpu_custom_call" | custom-call | flops 805306368 | bytes 10485760 | tf_op jit(solution)/shard_map/partial_scores/pallas_call | solution.py:216
  199.0 2.4 %collective-permute-start.9 = (f32[4,128,512]{2,1,0:T(8,128)S(1)}, f32[4,128,512]{2,1,0:T(8,128)S(1)}, u32[]{:S(2)}, u32[]{:S(2)}) collective-permute-start(f32[4,128,512]{2,1,0:T(8,128)S(1)} %get-tuple-element.19.refs_0_), channel_id=1, source_target_pairs={{0,1},{1,0},{2,3},{3,2},{4,5},{5,4},{6,7},{7,6},{8,9},{9,8},{10,11... | collective-permute-start | bytes 3145736 | tf_op jit(solution)/shard_map/ppermute | solution.py:373
  201.4 2.3 %collective-permute-done.9.refs_1_ = f32[4,128,512]{2,1,0:T(8,128)S(1)} collective-permute-done((f32[4,128,512]{2,1,0:T(8,128)S(1)}, f32[4,128,512]{2,1,0:T(8,128)S(1)}, u32[]{:S(2)}, u32[]{:S(2)}) %collective-permute-start.9) | collective-permute-done | bytes 1048608 | tf_op jit(solution)/shard_map/ppermute | solution.py:373
  203.7 4.2 %losses_and_gradients.1 = (f32[2,1,128]{2,1,0:T(1,128)}, bf16[512,2048]{1,0:T(8,128)(2,1)}) custom-call(s32[1]{0:T(128)} %bitcast.1.share_ref, f32[4,128,512]{2,1,0:T(8,128)S(1)} %get-tuple-element.19.refs_0_, f32[4,128,512]{2,1,0:T(8,128)S(1)} %collective-permute-done.9.refs_1_, bf16[16,128,2048]{2,1,0:T(8,128)(2,1)S(1)} %get-tuple-element.20.refs_2_, ...), custom_call_target="tpu_custom_call" | custom-call | flops 1073741824 | bytes 2097152 | tf_op jit(solution)/shard_map/losses_and_gradients/pallas_call | solution.py:283
  (14 shorter events, 0.2 us)
Async XLA Ops:
  0.6 16.4 %copy-start.6 = (s32[16]{0:T(128)S(1)}, s32[16]{0:T(128)}, u32[]{:S(2)}) copy-start(s32[16]{0:T(128)} %constant.126) | copy-start | bytes 196
  1.6 14.1 %collective-permute-start = (bf16[1024,128]{1,0:T(8,128)(2,1)S(1)}, bf16[1024,128]{1,0:T(8,128)(2,1)S(1)}, u32[]{:S(2)}, u32[]{:S(2)}) collective-permute-start(bf16[1024,128]{1,0:T(8,128)(2,1)S(1)} %slice.31), channel_id=1, source_target_pairs={{0,24},{2,26},{4,28},{6,30},{8,16},{10,18},{12,20},{14,22},{16,8},... | collective-permute-start | bytes 786440 | tf_op jit(solution)/shard_map/ppermute | solution.py:323
  4.5 10.9 %all-to-all-start = ((s32[16,1,1]{2,1,0:T(1,128)}), s32[16,1,1]{2,1,0:T(1,128)S(1)}, u32[]{:S(2)}, u32[]{:S(2)}) async-start(s32[16,1,1]{2,1,0:T(1,128)} %copy.20), calls=%async_computation | async-start | bytes 16384 | tf_op jit(solution)/shard_map/all_to_all | solution.py:332
  15.8 9.4 %copy-start.8 = (bf16[1024,128]{1,0:T(8,128)(2,1)}, bf16[1024,128]{1,0:T(8,128)(2,1)S(1)}, u32[]{:S(2)}) copy-start(bf16[1024,128]{1,0:T(8,128)(2,1)S(1)} %collective-permute-done.refs_0_) | copy-start | bytes 786436
  15.8 34.6 %collective-permute-start.1 = (bf16[1024,384]{1,0:T(8,128)(2,1)S(1)}, bf16[1024,384]{1,0:T(8,128)(2,1)S(1)}, u32[]{:S(2)}, u32[]{:S(2)}) collective-permute-start(bf16[1024,384]{1,0:T(8,128)(2,1)S(1)} %slice.30), channel_id=1, source_target_pairs={{0,24},{2,26},{4,28},{6,30},{8,16},{10,18},{12,20},{14,22},{16,8},... | collective-permute-start | bytes 2359304 | tf_op jit(solution)/shard_map/ppermute | solution.py:336
  25.1 168.9 %all-to-all-start.1 = ((bf16[16,128,1536]{2,1,0:T(8,128)(2,1)}), bf16[16,128,1536]{2,1,0:T(8,128)(2,1)}, u32[]{:S(2)}, u32[]{:S(2)}) async-start(bf16[16,128,1536]{2,1,0:T(8,128)(2,1)} %pick_blocks.1), calls=%async_computation.1 | async-start | bytes 12582912 | tf_op jit(solution)/shard_map/all_to_all | solution.py:343
  50.4 0.9 copy-start.7
  53.9 1.3 copy-start.1
  55.3 2.1 copy-start.5
  55.3 2.1 copy-start.3
  56.3 23.3 %collective-permute-start.2 = (bf16[2,128,512]{2,1,0:T(8,128)(2,1)}, bf16[2,128,512]{2,1,0:T(8,128)(2,1)}, u32[]{:S(2)}, u32[]{:S(2)}) collective-permute-start(bf16[2,128,512]{2,1,0:T(8,128)(2,1)} %get-tuple-element.34), channel_id=1, source_target_pairs={{0,2},{2,4},{4,6},{6,8},{8,10},{10,12},{12,14},{14,0},{16,18},{18,... | collective-permute-start | bytes 786440 | tf_op jit(solution)/shard_map/ppermute | solution.py:355
  58.1 101.6 %collective-permute-start.4 = (bf16[2,128,512]{2,1,0:T(8,128)(2,1)S(1)}, bf16[2,128,512]{2,1,0:T(8,128)(2,1)S(1)}, u32[]{:S(2)}, u32[]{:S(2)}) collective-permute-start(bf16[2,128,512]{2,1,0:T(8,128)(2,1)S(1)} %get-tuple-element.32), channel_id=1, source_target_pairs={{0,6},{2,8},{4,10},{6,12},{8,14},{10,0},{12,2},{14,4},{16,22},{18,... | collective-permute-start | bytes 786440 | tf_op jit(solution)/shard_map/ppermute | solution.py:355
  58.1 115.3 %copy-start = (bf16[512,2048]{1,0:T(8,128)(2,1)S(1)}, bf16[512,2048]{1,0:T(8,128)(2,1)}, u32[]{:S(2)}) copy-start(bf16[512,2048]{1,0:T(8,128)(2,1)} %query_ref.3) | copy-start | bytes 6291460
  58.1 101.5 %collective-permute-start.3 = (bf16[2,128,512]{2,1,0:T(8,128)(2,1)}, bf16[2,128,512]{2,1,0:T(8,128)(2,1)S(1)}, u32[]{:S(2)}, u32[]{:S(2)}) collective-permute-start(bf16[2,128,512]{2,1,0:T(8,128)(2,1)} %get-tuple-element.33), channel_id=1, source_target_pairs={{0,4},{2,6},{4,8},{6,10},{8,12},{10,14},{12,0},{14,2},{16,20},{18,... | collective-permute-start | bytes 786440 | tf_op jit(solution)/shard_map/ppermute | solution.py:355
  59.3 112.7 %collective-permute-start.8 = (bf16[2,128,512]{2,1,0:T(8,128)(2,1)S(1)}, bf16[2,128,512]{2,1,0:T(8,128)(2,1)S(1)}, u32[]{:S(2)}, u32[]{:S(2)}) collective-permute-start(bf16[2,128,512]{2,1,0:T(8,128)(2,1)S(1)} %get-tuple-element.28), channel_id=1, source_target_pairs={{0,14},{2,0},{4,2},{6,4},{8,6},{10,8},{12,10},{14,12},{16,30},{18,... | collective-permute-start | bytes 786440 | tf_op jit(solution)/shard_map/ppermute | solution.py:355
  60.4 111.6 %collective-permute-start.7 = (bf16[2,128,512]{2,1,0:T(8,128)(2,1)S(1)}, bf16[2,128,512]{2,1,0:T(8,128)(2,1)S(1)}, u32[]{:S(2)}, u32[]{:S(2)}) collective-permute-start(bf16[2,128,512]{2,1,0:T(8,128)(2,1)S(1)} %get-tuple-element.29), channel_id=1, source_target_pairs={{0,12},{2,14},{4,0},{6,2},{8,4},{10,6},{12,8},{14,10},{16,28},{18,... | collective-permute-start | bytes 786440 | tf_op jit(solution)/shard_map/ppermute | solution.py:355
  79.6 80.9 %collective-permute-start.5 = (bf16[2,128,512]{2,1,0:T(8,128)(2,1)S(1)}, bf16[2,128,512]{2,1,0:T(8,128)(2,1)S(1)}, u32[]{:S(2)}, u32[]{:S(2)}) collective-permute-start(bf16[2,128,512]{2,1,0:T(8,128)(2,1)S(1)} %get-tuple-element.31), channel_id=1, source_target_pairs={{0,8},{2,10},{4,12},{6,14},{8,0},{10,2},{12,4},{14,6},{16,24},{18,... | collective-permute-start | bytes 786440 | tf_op jit(solution)/shard_map/ppermute | solution.py:355
  159.7 12.3 %collective-permute-start.6 = (bf16[2,128,512]{2,1,0:T(8,128)(2,1)S(1)}, bf16[2,128,512]{2,1,0:T(8,128)(2,1)S(1)}, u32[]{:S(2)}, u32[]{:S(2)}) collective-permute-start(bf16[2,128,512]{2,1,0:T(8,128)(2,1)S(1)} %get-tuple-element.30), channel_id=1, source_target_pairs={{0,10},{2,12},{4,14},{6,0},{8,2},{10,4},{12,6},{14,8},{16,26},{18,... | collective-permute-start | bytes 786440 | tf_op jit(solution)/shard_map/ppermute | solution.py:355
  172.1 1.3 copy-start.4
  173.4 20.7 %copy-start.2 = (s32[512]{0:T(512)S(1)}, s32[512]{0:T(512)}, u32[]{:S(2)}) copy-start(s32[512]{0:T(512)} %param.9) | copy-start | bytes 6148
  199.0 4.7 %collective-permute-start.9 = (f32[4,128,512]{2,1,0:T(8,128)S(1)}, f32[4,128,512]{2,1,0:T(8,128)S(1)}, u32[]{:S(2)}, u32[]{:S(2)}) collective-permute-start(f32[4,128,512]{2,1,0:T(8,128)S(1)} %get-tuple-element.19.refs_0_), channel_id=1, source_target_pairs={{0,1},{1,0},{2,3},{3,2},{4,5},{5,4},{6,7},{7,6},{8,9},{9,8},{10,11... | collective-permute-start | bytes 3145736 | tf_op jit(solution)/shard_map/ppermute | solution.py:373

commit v4 on v3

--- a/solution.py
+++ b/solution.py
@@ -312,41 +312,41 @@
     half = dp_count // 2
     me = lax.axis_index("dp")
     me_in_half = me % half
+    share = lax.axis_index("fsdp").astype(jnp.int32)
+    cand_blocks, share = lax.optimization_barrier((cand_blocks, share))
     owners = cand_blocks // passage_blocks
     local_ids = cand_blocks % passage_blocks
 
-    share = lax.axis_index("fsdp").astype(jnp.int32)
     far = half + half // 2
     to_other_half = [(d, d ^ far) for d in range(dp_count)]
     first = LANES
     swapped = first + max(1, feature_count // LANES * 3 // 16) * LANES
     early_half = lax.ppermute(passage_emb[:, :first], "dp", to_other_half)
 
-    owner_index = lax.broadcasted_iota(jnp.int32, (dp_count, query_blocks, list_len), 0)
-    other_half = (owner_index ^ far) == owners[None]
-    both_ids = jnp.where(owner_index == owners[None], local_ids[None], 0) + jnp.where(
-        other_half, SHIFT * local_ids[None], 0
-    )
-    both_tables = jnp.sum(both_ids, axis=(1, 2)).reshape(dp_count, 1)
-    both_tables, share = lax.optimization_barrier((both_tables, share))
-    requested = lax.all_to_all(both_tables, "dp", split_axis=0, concat_axis=0, tiled=True)
-    requested = requested.reshape(dp_count)
+    quarter = dp_count // 4
+    order = [quarter * z + c for c in range(quarter) for z in (0, 3, 1, 2)]
+    places = jnp.asarray([order.index(d) for d in range(dp_count)], jnp.int32)
+
+    def all_to_all(array):
+        return lax.all_to_all(
+            array, "dp", split_axis=0, concat_axis=0, tiled=True, axis_index_groups=[order]
+        )
+
+    member = jnp.asarray(order, jnp.int32)[:, None, None]
+    both_ids = jnp.where(member == owners[None], local_ids[None], 0) + jnp.where(
+        (member ^ far) == owners[None], SHIFT * local_ids[None], 0
+    )
+    requested = all_to_all(jnp.sum(both_ids, axis=(1, 2)).reshape(dp_count, 1)).reshape(dp_count)
     requested, early_half = lax.optimization_barrier((requested, early_half))
     late_half, requested = lax.optimization_barrier((passage_emb[:, first:swapped], requested))
     far_parts = [early_half, lax.ppermute(late_half, "dp", to_other_half)]
-    quarter = dp_count // 4
-    order = [quarter * z + c for c in range(quarter) for z in (0, 3, 1, 2)]
-    slots = jnp.asarray([order.index(d) for d in range(dp_count)], jnp.int32)[owners]
-    picked = pick_blocks(
-        (requested % SHIFT)[jnp.asarray(order, jnp.int32)], passage_emb, block_rows, swapped
-    )
-    fetched = lax.all_to_all(
-        picked, "dp", split_axis=0, concat_axis=0, tiled=True, axis_index_groups=[order]
-    )
+    picked = pick_blocks(requested % SHIFT, passage_emb, block_rows, swapped)
+    fetched = all_to_all(picked)
 
     steps = jnp.arange(half, dtype=jnp.int32)
     readers = me - me_in_half + (me_in_half + steps) % half
-    relayed = requested[readers]
+    requested, far_parts[1] = lax.optimization_barrier((requested, far_parts[1]))
+    relayed = requested[places[readers]]
     relayed = jnp.stack([relayed % SHIFT, relayed // SHIFT], axis=1)
     pairs = pick_pairs(relayed, passage_emb, far_parts, block_rows)
     near = jnp.concatenate(
@@ -367,7 +367,7 @@
 
     before = near_scores(near_slots, query_emb, near)
     mine, listed, positive = partial_scores(
-        near_slots, slots, query_emb, positive, before, near, fetched
+        near_slots, places[owners], query_emb, positive, before, near, fetched
     )
     scores = [mine] + [
         lax.ppermute(mine, "fsdp", [(i, (i + k) % fsdp_count) for i in range(fsdp_count)])

time: 208 us -> 207 us (level)
    unnamed x25 -> x29, local copies, waits for them, and re-layouts: 5.7 us -> 4.95 us
  transfers between devices with their start and end apart: 12 -> 12, of which waited for: 8 -> 8; matrix products, arithmetic and copies ran while one was open for 4% -> 5% of each run, Pallas kernels for 6% -> 6%
where the time goes in v4:
time: 207 us
  waiting for transfers between devices  149 us (72%)
  starting transfers between devices  22.8 us (11%)
  Pallas kernels  20.5 us (10%)
  local copies, waits for them, and re-layouts  11.1 us (5%)
  other arithmetic  2.52 us (1%)
    ppermute x7, waiting for transfers between devices, shards(): lax.ppermute(pairs[k], 'dp', [(d, d - d % half + (d % half + k) % half) f...  108 us
    all_to_all x2, waiting for transfers between devices, all_to_all(): lax.all_to_all(array, 'dp', split_axis=0, concat_axis=0, tiled=True, axis...  20.6 us
    ppermute x1, waiting for transfers between devices, shards(): far_parts = [early_half, lax.ppermute(late_half, 'dp', to_other_half)]  18.6 us
    all_to_all x2, starting transfers between devices, all_to_all(): lax.all_to_all(array, 'dp', split_axis=0, concat_axis=0, tiled=True, axis...  13 us
    pallas_call x1, Pallas kernels, pick_blocks(): pl.pallas_call(pick_kernel, out_shape=pltpu.HBM((count, block_rows, featu...  5.99 us
    unnamed x29, local copies, waits for them, and re-layouts  4.95 us
    pallas_call x1, Pallas kernels, partial_scores(): pl.pallas_call(score_kernel, out_shape=(pltpu.VMEM((query_blocks, block_r...  4.91 us
    ppermute x7, starting transfers between devices, shards(): lax.ppermute(pairs[k], 'dp', [(d, d - d % half + (d % half + k) % half) f...  4.83 us
  transfers between devices with their start and end apart: 12, of which 8 were waited for; matrix products, arithmetic and copies ran while one was open for 5% of the time, Pallas kernels for 6%

profile of v4, /device:TPU:11, one launch (start us, length us, event | category | flops | bytes accessed | tf_op | source)
XLA Modules:
  0.0 206.9 jit_solution(1105998966876915270)
XLA Ops:
  0.6 0.0 copy-start.3
  0.6 1.0 slice.31
  1.6 1.4 collective-permute-start
  3.0 0.7 broadcast_multiply_fusion
  3.7 0.0 copy-start.6
  3.7 0.8 add_reduce_fusion
  4.4 0.7 copy.26
  5.1 5.6 %all-to-all-start = ((s32[16,1,1]{2,1,0:T(1,128)}), s32[16,1,1]{2,1,0:T(1,128)S(1)}, u32[]{:S(2)}, u32[]{:S(2)}) async-start(s32[16,1,1]{2,1,0:T(1,128)} %copy.26), calls=%async_computation | async-start | bytes 16384 | tf_op jit(solution)/shard_map/all_to_all | solution.py:331
  10.8 1.2 slice.30
  12.0 0.0 copy-done.6
  12.0 3.4 %all-to-all-done = s32[16,1,1]{2,1,0:T(1,128)S(1)} async-done(((s32[16,1,1]{2,1,0:T(1,128)}), s32[16,1,1]{2,1,0:T(1,128)S(1)}, u32[]{:S(2)}, u32[]{:S(2)}) %all-to-all-start) | async-done | bytes 96 | tf_op jit(solution)/shard_map/all_to_all | solution.py:331
  15.4 0.4 reduce
  15.8 0.0 collective-permute-done.refs_0_
  15.8 0.0 copy-start.10
  15.8 1.2 collective-permute-start.1
  17.0 0.1 reshape.171
  17.1 0.0 copy-done.3
  17.1 0.6 gather_fusion.1
  17.8 0.6 pad_clamp_fusion
  18.4 6.0 %pick_blocks.1 = bf16[16,128,1536]{2,1,0:T(8,128)(2,1)} custom-call(s32[16]{0:T(128)S(1)} %and_select_fusion.ids_ref, bf16[1024,2048]{1,0:T(8,128)(2,1)} %stored_ref.3), custom_call_target="tpu_custom_call" | custom-call | bytes 12582912 | tf_op jit(solution)/shard_map/pick_blocks/pallas_call | solution.py:65
  24.4 0.0 copy-done.10
  24.4 7.4 %all-to-all-start.1 = ((bf16[16,128,1536]{2,1,0:T(8,128)(2,1)}), bf16[16,128,1536]{2,1,0:T(8,128)(2,1)}, u32[]{:S(2)}, u32[]{:S(2)}) async-start(bf16[16,128,1536]{2,1,0:T(8,128)(2,1)} %pick_blocks.1), calls=%async_computation.1 | async-start | bytes 12582912 | tf_op jit(solution)/shard_map/all_to_all | solution.py:331
  31.8 18.6 %collective-permute-done.1.refs_1_ = bf16[1024,384]{1,0:T(8,128)(2,1)S(1)} collective-permute-done((bf16[1024,384]{1,0:T(8,128)(2,1)S(1)}, bf16[1024,384]{1,0:T(8,128)(2,1)S(1)}, u32[]{:S(2)}, u32[]{:S(2)}) %collective-permute-start.1) | collective-permute-done | bytes 786464 | tf_op jit(solution)/shard_map/ppermute | solution.py:342
  50.4 0.0 copy-start.9
  50.4 0.6 gather_fusion.2
  51.1 0.1 copy.27.ids_ref
  51.2 0.1 copy-done.9
  51.3 2.4 %pick_pairs.1 = bf16[8,2,128,512]{3,2,1,0:T(8,128)(2,1)S(1)} custom-call(s32[8,2]{1,0:T(8,128)S(1)} %copy.27.ids_ref, bf16[1024,2048]{1,0:T(8,128)(2,1)} %stored_ref.3, bf16[1024,128]{1,0:T(8,128)(2,1)} %copy-done.10, bf16[1024,384]{1,0:T(8,128)(2,1)} %copy-done.9), custom_call_target="tpu_custom_call" | custom-call | flops 999999995904 | bytes 1000000000 | tf_op jit(solution)/shard_map/pick_pairs/pallas_call | solution.py:110
  53.7 0.0 copy-start.1
  53.7 1.3 copy-done.1
  55.1 0.0 copy-start.7
  55.1 0.0 copy-start.4
  55.1 1.0 slice_bitcast_fusion
  56.1 1.2 collective-permute-start.2
  57.3 0.0 copy-done.7
  57.3 0.0 copy-done.4
  57.3 0.0 copy-done.8
  57.3 0.7 gather_fusion
  58.0 0.1 reshape.170.slots_ref
  58.1 0.0 collective-permute-start.4
  58.1 0.1 collective-permute-start.3
  58.2 1.1 fusion
  59.3 1.2 collective-permute-start.8
  60.5 2.3 %collective-permute-start.7 = (bf16[2,128,512]{2,1,0:T(8,128)(2,1)S(1)}, bf16[2,128,512]{2,1,0:T(8,128)(2,1)S(1)}, u32[]{:S(2)}, u32[]{:S(2)}) collective-permute-start(bf16[2,128,512]{2,1,0:T(8,128)(2,1)S(1)} %get-tuple-element.33), channel_id=1, source_target_pairs={{0,12},{2,14},{4,0},{6,2},{8,4},{10,6},{12,8},{14,10},{16,28},{18,... | collective-permute-start | bytes 786440 | tf_op jit(solution)/shard_map/ppermute | solution.py:355
  62.8 15.9 %collective-permute-done.2 = bf16[2,128,512]{2,1,0:T(8,128)(2,1)} collective-permute-done((bf16[2,128,512]{2,1,0:T(8,128)(2,1)}, bf16[2,128,512]{2,1,0:T(8,128)(2,1)}, u32[]{:S(2)}, u32[]{:S(2)}) %collective-permute-start.2) | collective-permute-done | bytes 262176 | tf_op jit(solution)/shard_map/ppermute | solution.py:355
  78.7 0.0 collective-permute-start.5
  78.7 1.0 constant_dynamic-update-slice_fusion.6
  79.7 79.3 %collective-permute-done.3 = bf16[2,128,512]{2,1,0:T(8,128)(2,1)S(1)} collective-permute-done((bf16[2,128,512]{2,1,0:T(8,128)(2,1)}, bf16[2,128,512]{2,1,0:T(8,128)(2,1)S(1)}, u32[]{:S(2)}, u32[]{:S(2)}) %collective-permute-start.3) | collective-permute-done | bytes 262176 | tf_op jit(solution)/shard_map/ppermute | solution.py:355
  159.0 0.0 collective-permute-start.6
  159.0 0.0 collective-permute-done.4
  159.1 2.2 %collective-permute-done.5 = bf16[2,128,512]{2,1,0:T(8,128)(2,1)S(1)} collective-permute-done((bf16[2,128,512]{2,1,0:T(8,128)(2,1)S(1)}, bf16[2,128,512]{2,1,0:T(8,128)(2,1)S(1)}, u32[]{:S(2)}, u32[]{:S(2)}) %collective-permute-start.5) | collective-permute-done | bytes 262176 | tf_op jit(solution)/shard_map/ppermute | solution.py:355
  161.2 10.2 %collective-permute-done.6 = bf16[2,128,512]{2,1,0:T(8,128)(2,1)S(1)} collective-permute-done((bf16[2,128,512]{2,1,0:T(8,128)(2,1)S(1)}, bf16[2,128,512]{2,1,0:T(8,128)(2,1)S(1)}, u32[]{:S(2)}, u32[]{:S(2)}) %collective-permute-start.6) | collective-permute-done | bytes 262176 | tf_op jit(solution)/shard_map/ppermute | solution.py:355
  171.5 0.0 collective-permute-done.7
  171.5 0.0 collective-permute-done.8
  171.5 0.0 copy-start.5
  171.6 1.3 copy-done.5
  172.9 0.0 copy-done
  172.9 3.0 %near_scores.1.before_ref = f32[4,128,512]{2,1,0:T(8,128)S(1)} custom-call(s32[4,4]{1,0:T(4,128)S(1)} %fusion.5.near_slots_ref, bf16[512,2048]{1,0:T(8,128)(2,1)S(1)} %copy-done, bf16[16,128,512]{2,1,0:T(8,128)(2,1)} %copy-done.5), custom_call_target="tpu_custom_call" | custom-call | flops 268435456 | bytes 4194304 | tf_op jit(solution)/shard_map/near_scores/pallas_call | solution.py:165
  175.9 17.2 %all-to-all-done.1.fetched_ref = bf16[16,128,1536]{2,1,0:T(8,128)(2,1)} async-done(((bf16[16,128,1536]{2,1,0:T(8,128)(2,1)}), bf16[16,128,1536]{2,1,0:T(8,128)(2,1)}, u32[]{:S(2)}, u32[]{:S(2)}) %all-to-all-start.1) | async-done | bytes 6291488 | tf_op jit(solution)/shard_map/all_to_all | solution.py:331
  193.1 0.0 copy-done.2
  193.1 4.9 %partial_scores.1 = (f32[4,128,512]{2,1,0:T(8,128)S(1)}, bf16[16,128,2048]{2,1,0:T(8,128)(2,1)S(1)}, s32[4,1,128]{2,1,0:T(1,128)S(1)}) custom-call(s32[4,4]{1,0:T(4,128)S(1)} %fusion.5.near_slots_ref, s32[4,4]{1,0:T(4,128)S(1)} %reshape.170.slots_ref, bf16[512,2048]{1,0:T(8,128)(2,1)S(1)} %copy-done, s32[4,1,128]{2,1,0:T(1,128)S(1)} %bitcast.43, ...), custom_call_target="tpu_custom_call" | custom-call | flops 805306368 | bytes 10485760 | tf_op jit(solution)/shard_map/partial_scores/pallas_call | solution.py:216
  198.0 2.4 %collective-permute-start.9 = (f32[4,128,512]{2,1,0:T(8,128)S(1)}, f32[4,128,512]{2,1,0:T(8,128)S(1)}, u32[]{:S(2)}, u32[]{:S(2)}) collective-permute-start(f32[4,128,512]{2,1,0:T(8,128)S(1)} %get-tuple-element.23.refs_0_), channel_id=1, source_target_pairs={{0,1},{1,0},{2,3},{3,2},{4,5},{5,4},{6,7},{7,6},{8,9},{9,8},{10,11... | collective-permute-start | bytes 3145736 | tf_op jit(solution)/shard_map/ppermute | solution.py:373
  200.5 2.3 %collective-permute-done.9.refs_1_ = f32[4,128,512]{2,1,0:T(8,128)S(1)} collective-permute-done((f32[4,128,512]{2,1,0:T(8,128)S(1)}, f32[4,128,512]{2,1,0:T(8,128)S(1)}, u32[]{:S(2)}, u32[]{:S(2)}) %collective-permute-start.9) | collective-permute-done | bytes 1048608 | tf_op jit(solution)/shard_map/ppermute | solution.py:373
  202.7 4.2 %losses_and_gradients.1 = (f32[2,1,128]{2,1,0:T(1,128)}, bf16[512,2048]{1,0:T(8,128)(2,1)}) custom-call(s32[1]{0:T(128)} %bitcast.share_ref, f32[4,128,512]{2,1,0:T(8,128)S(1)} %get-tuple-element.23.refs_0_, f32[4,128,512]{2,1,0:T(8,128)S(1)} %collective-permute-done.9.refs_1_, bf16[16,128,2048]{2,1,0:T(8,128)(2,1)S(1)} %get-tuple-element.24.refs_2_, ...), custom_call_target="tpu_custom_call" | custom-call | flops 1073741824 | bytes 2097152 | tf_op jit(solution)/shard_map/losses_and_gradients/pallas_call | solution.py:283
  (16 shorter events, 0.2 us)
Async XLA Ops:
  0.6 16.5 %copy-start.3 = (s32[16]{0:T(128)S(1)}, s32[16]{0:T(128)}, u32[]{:S(2)}) copy-start(s32[16]{0:T(128)} %constant.117.clone) | copy-start | bytes 196
  1.6 14.1 %collective-permute-start = (bf16[1024,128]{1,0:T(8,128)(2,1)S(1)}, bf16[1024,128]{1,0:T(8,128)(2,1)S(1)}, u32[]{:S(2)}, u32[]{:S(2)}) collective-permute-start(bf16[1024,128]{1,0:T(8,128)(2,1)S(1)} %slice.31), channel_id=1, source_target_pairs={{0,24},{2,26},{4,28},{6,30},{8,16},{10,18},{12,20},{14,22},{16,8},... | collective-permute-start | bytes 786440 | tf_op jit(solution)/shard_map/ppermute | solution.py:324
  3.7 8.3 %copy-start.6 = (s32[4,4]{1,0:T(4,128)}, s32[4,4]{1,0:T(4,128)S(1)}, u32[]{:S(2)}) copy-start(s32[4,4]{1,0:T(4,128)S(1)} %get-tuple-element.40) | copy-start | bytes 196
  5.1 10.2 %all-to-all-start = ((s32[16,1,1]{2,1,0:T(1,128)}), s32[16,1,1]{2,1,0:T(1,128)S(1)}, u32[]{:S(2)}, u32[]{:S(2)}) async-start(s32[16,1,1]{2,1,0:T(1,128)} %copy.26), calls=%async_computation | async-start | bytes 16384 | tf_op jit(solution)/shard_map/all_to_all | solution.py:331
  15.8 8.6 %copy-start.10 = (bf16[1024,128]{1,0:T(8,128)(2,1)}, bf16[1024,128]{1,0:T(8,128)(2,1)S(1)}, u32[]{:S(2)}) copy-start(bf16[1024,128]{1,0:T(8,128)(2,1)S(1)} %collective-permute-done.refs_0_) | copy-start | bytes 786436
  15.8 34.6 %collective-permute-start.1 = (bf16[1024,384]{1,0:T(8,128)(2,1)S(1)}, bf16[1024,384]{1,0:T(8,128)(2,1)S(1)}, u32[]{:S(2)}, u32[]{:S(2)}) collective-permute-start(bf16[1024,384]{1,0:T(8,128)(2,1)S(1)} %slice.30), channel_id=1, source_target_pairs={{0,24},{2,26},{4,28},{6,30},{8,16},{10,18},{12,20},{14,22},{16,8},... | collective-permute-start | bytes 2359304 | tf_op jit(solution)/shard_map/ppermute | solution.py:342
  24.4 168.7 %all-to-all-start.1 = ((bf16[16,128,1536]{2,1,0:T(8,128)(2,1)}), bf16[16,128,1536]{2,1,0:T(8,128)(2,1)}, u32[]{:S(2)}, u32[]{:S(2)}) async-start(bf16[16,128,1536]{2,1,0:T(8,128)(2,1)} %pick_blocks.1), calls=%async_computation.1 | async-start | bytes 12582912 | tf_op jit(solution)/shard_map/all_to_all | solution.py:331
  50.4 0.9 copy-start.9
  53.7 1.3 copy-start.1
  55.1 2.3 %copy-start.7 = (s32[4,4]{1,0:T(4,128)S(1)}, s32[4,4]{1,0:T(4,128)}, u32[]{:S(2)}) copy-start(s32[4,4]{1,0:T(4,128)} %copy-done.6) | copy-start | bytes 196
  55.1 2.3 %copy-start.4 = (s32[16]{0:T(128)S(1)}, s32[16]{0:T(128)}, u32[]{:S(2)}) copy-start(s32[16]{0:T(128)} %constant.117.clone) | copy-start | bytes 196
  55.1 2.3 %copy-start.8 = (s32[1024]{0:T(1024)S(1)}, s32[1024]{0:T(1024)}, u32[]{:S(2)}) copy-start(s32[1024]{0:T(1024)} %get-tuple-element.44) | copy-start | bytes 12292
  56.1 22.6 %collective-permute-start.2 = (bf16[2,128,512]{2,1,0:T(8,128)(2,1)}, bf16[2,128,512]{2,1,0:T(8,128)(2,1)}, u32[]{:S(2)}, u32[]{:S(2)}) collective-permute-start(bf16[2,128,512]{2,1,0:T(8,128)(2,1)} %get-tuple-element.38), channel_id=1, source_target_pairs={{0,2},{2,4},{4,6},{6,8},{8,10},{10,12},{12,14},{14,0},{16,18},{18,... | collective-permute-start | bytes 786440 | tf_op jit(solution)/shard_map/ppermute | solution.py:355
  58.1 100.9 %collective-permute-start.4 = (bf16[2,128,512]{2,1,0:T(8,128)(2,1)S(1)}, bf16[2,128,512]{2,1,0:T(8,128)(2,1)S(1)}, u32[]{:S(2)}, u32[]{:S(2)}) collective-permute-start(bf16[2,128,512]{2,1,0:T(8,128)(2,1)S(1)} %get-tuple-element.36), channel_id=1, source_target_pairs={{0,6},{2,8},{4,10},{6,12},{8,14},{10,0},{12,2},{14,4},{16,22},{18,... | collective-permute-start | bytes 786440 | tf_op jit(solution)/shard_map/ppermute | solution.py:355
  58.1 114.8 %copy-start = (bf16[512,2048]{1,0:T(8,128)(2,1)S(1)}, bf16[512,2048]{1,0:T(8,128)(2,1)}, u32[]{:S(2)}) copy-start(bf16[512,2048]{1,0:T(8,128)(2,1)} %query_ref.3) | copy-start | bytes 6291460
  58.1 100.9 %collective-permute-start.3 = (bf16[2,128,512]{2,1,0:T(8,128)(2,1)}, bf16[2,128,512]{2,1,0:T(8,128)(2,1)S(1)}, u32[]{:S(2)}, u32[]{:S(2)}) collective-permute-start(bf16[2,128,512]{2,1,0:T(8,128)(2,1)} %get-tuple-element.37), channel_id=1, source_target_pairs={{0,4},{2,6},{4,8},{6,10},{8,12},{10,14},{12,0},{14,2},{16,20},{18,... | collective-permute-start | bytes 786440 | tf_op jit(solution)/shard_map/ppermute | solution.py:355
  59.3 112.2 %collective-permute-start.8 = (bf16[2,128,512]{2,1,0:T(8,128)(2,1)S(1)}, bf16[2,128,512]{2,1,0:T(8,128)(2,1)S(1)}, u32[]{:S(2)}, u32[]{:S(2)}) collective-permute-start(bf16[2,128,512]{2,1,0:T(8,128)(2,1)S(1)} %get-tuple-element.32), channel_id=1, source_target_pairs={{0,14},{2,0},{4,2},{6,4},{8,6},{10,8},{12,10},{14,12},{16,30},{18,... | collective-permute-start | bytes 786440 | tf_op jit(solution)/shard_map/ppermute | solution.py:355
  60.5 111.0 %collective-permute-start.7 = (bf16[2,128,512]{2,1,0:T(8,128)(2,1)S(1)}, bf16[2,128,512]{2,1,0:T(8,128)(2,1)S(1)}, u32[]{:S(2)}, u32[]{:S(2)}) collective-permute-start(bf16[2,128,512]{2,1,0:T(8,128)(2,1)S(1)} %get-tuple-element.33), channel_id=1, source_target_pairs={{0,12},{2,14},{4,0},{6,2},{8,4},{10,6},{12,8},{14,10},{16,28},{18,... | collective-permute-start | bytes 786440 | tf_op jit(solution)/shard_map/ppermute | solution.py:355
  78.7 82.5 %collective-permute-start.5 = (bf16[2,128,512]{2,1,0:T(8,128)(2,1)S(1)}, bf16[2,128,512]{2,1,0:T(8,128)(2,1)S(1)}, u32[]{:S(2)}, u32[]{:S(2)}) collective-permute-start(bf16[2,128,512]{2,1,0:T(8,128)(2,1)S(1)} %get-tuple-element.35), channel_id=1, source_target_pairs={{0,8},{2,10},{4,12},{6,14},{8,0},{10,2},{12,4},{14,6},{16,24},{18,... | collective-permute-start | bytes 786440 | tf_op jit(solution)/shard_map/ppermute | solution.py:355
  159.0 12.4 %collective-permute-start.6 = (bf16[2,128,512]{2,1,0:T(8,128)(2,1)S(1)}, bf16[2,128,512]{2,1,0:T(8,128)(2,1)S(1)}, u32[]{:S(2)}, u32[]{:S(2)}) collective-permute-start(bf16[2,128,512]{2,1,0:T(8,128)(2,1)S(1)} %get-tuple-element.34), channel_id=1, source_target_pairs={{0,10},{2,12},{4,14},{6,0},{8,2},{10,4},{12,6},{14,8},{16,26},{18,... | collective-permute-start | bytes 786440 | tf_op jit(solution)/shard_map/ppermute | solution.py:355
  171.5 1.3 copy-start.5
  172.9 20.3 %copy-start.2 = (s32[512]{0:T(512)S(1)}, s32[512]{0:T(512)}, u32[]{:S(2)}) copy-start(s32[512]{0:T(512)} %param.9) | copy-start | bytes 6148
  198.0 4.7 %collective-permute-start.9 = (f32[4,128,512]{2,1,0:T(8,128)S(1)}, f32[4,128,512]{2,1,0:T(8,128)S(1)}, u32[]{:S(2)}, u32[]{:S(2)}) collective-permute-start(f32[4,128,512]{2,1,0:T(8,128)S(1)} %get-tuple-element.23.refs_0_), channel_id=1, source_target_pairs={{0,1},{1,0},{2,3},{3,2},{4,5},{5,4},{6,7},{7,6},{8,9},{9,8},{10,11... | collective-permute-start | bytes 3145736 | tf_op jit(solution)/shard_map/ppermute | solution.py:373

commit v5 on v4

--- a/solution.py
+++ b/solution.py
@@ -337,8 +337,7 @@
         (member ^ far) == owners[None], SHIFT * local_ids[None], 0
     )
     requested = all_to_all(jnp.sum(both_ids, axis=(1, 2)).reshape(dp_count, 1)).reshape(dp_count)
-    requested, early_half = lax.optimization_barrier((requested, early_half))
-    late_half, requested = lax.optimization_barrier((passage_emb[:, first:swapped], requested))
+    late_half, early_half = lax.optimization_barrier((passage_emb[:, first:swapped], early_half))
     far_parts = [early_half, lax.ppermute(late_half, "dp", to_other_half)]
     picked = pick_blocks(requested % SHIFT, passage_emb, block_rows, swapped)
     fetched = all_to_all(picked)

time: 207 us -> 203 us (0.981); the launches traced: 207 us -> 199 us
  starting transfers between devices: 22.8 us -> 18.4 us
  waiting for transfers between devices: 149 us -> 146 us
    ppermute x7, waiting for transfers between devices: 108 us -> 79.1 us  [shards(): lax.ppermute(pairs[k], 'dp', [(d, d - d % half + (d % half + k) % half) f...]
    all_to_all x2, waiting for transfers between devices: 20.6 us -> 32.1 us  [all_to_all(): lax.all_to_all(array, 'dp', split_axis=0, concat_axis=0, tiled=True, axis...]
    ppermute x1, waiting for transfers between devices: 18.6 us -> 29.6 us  [shards(): far_parts = [early_half, lax.ppermute(late_half, 'dp', to_other_half)]]
    all_to_all x2, starting transfers between devices: 13 us -> 10.3 us  [all_to_all(): lax.all_to_all(array, 'dp', split_axis=0, concat_axis=0, tiled=True, axis...]
    ppermute x1, waiting for transfers between devices: 0.01 us -> 2.73 us  [shards(): early_half = lax.ppermute(passage_emb[:, :first], 'dp', to_other_half)]
  transfers between devices with their start and end apart: 12 -> 12, of which waited for: 8 -> 7; matrix products, arithmetic and copies ran while one was open for 5% -> 5% of each run, Pallas kernels for 6% -> 6%
where the time goes in v5:
time: 203 us; the launch traced here: 199 us
  waiting for transfers between devices  146 us (72%)
  Pallas kernels  20.6 us (10%)
  starting transfers between devices  18.4 us (9%)
  local copies, waits for them, and re-layouts  10.9 us (5%)
  other arithmetic  2.52 us (1%)
    ppermute x7, waiting for transfers between devices, shards(): lax.ppermute(pairs[k], 'dp', [(d, d - d % half + (d % half + k) % half) f...  79.1 us
    all_to_all x2, waiting for transfers between devices, all_to_all(): lax.all_to_all(array, 'dp', split_axis=0, concat_axis=0, tiled=True, axis...  32.1 us
    ppermute x1, waiting for transfers between devices, shards(): far_parts = [early_half, lax.ppermute(late_half, 'dp', to_other_half)]  29.6 us
    all_to_all x2, starting transfers between devices, all_to_all(): lax.all_to_all(array, 'dp', split_axis=0, concat_axis=0, tiled=True, axis...  10.3 us
    pallas_call x1, Pallas kernels, pick_blocks(): pl.pallas_call(pick_kernel, out_shape=pltpu.HBM((count, block_rows, featu...  6.02 us
    ppermute x7, starting transfers between devices, shards(): lax.ppermute(pairs[k], 'dp', [(d, d - d % half + (d % half + k) % half) f...  5.14 us
    pallas_call x1, Pallas kernels, partial_scores(): pl.pallas_call(score_kernel, out_shape=(pltpu.VMEM((query_blocks, block_r...  4.91 us
    unnamed x29, local copies, waits for them, and re-layouts  4.81 us
  transfers between devices with their start and end apart: 12, of which 7 were waited for; matrix products, arithmetic and copies ran while one was open for 5% of the time, Pallas kernels for 6%

profile of v5, /device:TPU:11, one launch (start us, length us, event | category | flops | bytes accessed | tf_op | source)
XLA Modules:
  0.0 199.0 jit_solution(13625950733514383666)
XLA Ops:
  0.6 0.0 copy-start.3
  0.6 1.0 slice.31
  1.6 1.4 collective-permute-start
  3.0 0.7 broadcast_multiply_fusion
  3.7 0.0 copy-start.6
  3.7 0.8 add_reduce_fusion
  4.4 0.7 copy.26
  5.1 0.0 copy-done.6
  5.1 5.6 %all-to-all-start = ((s32[16,1,1]{2,1,0:T(1,128)}), s32[16,1,1]{2,1,0:T(1,128)S(1)}, u32[]{:S(2)}, u32[]{:S(2)}) async-start(s32[16,1,1]{2,1,0:T(1,128)} %copy.26), calls=%async_computation | async-start | bytes 16384 | tf_op jit(solution)/shard_map/all_to_all | solution.py:331
  10.8 1.2 slice.30
  12.0 2.7 %collective-permute-done.refs_0_ = bf16[1024,128]{1,0:T(8,128)(2,1)S(1)} collective-permute-done((bf16[1024,128]{1,0:T(8,128)(2,1)S(1)}, bf16[1024,128]{1,0:T(8,128)(2,1)S(1)}, u32[]{:S(2)}, u32[]{:S(2)}) %collective-permute-start) | collective-permute-done | bytes 262176 | tf_op jit(solution)/shard_map/ppermute | solution.py:324
  14.7 0.0 copy-start.10
  14.7 1.2 collective-permute-start.1
  15.9 0.1 reshape.171
  16.0 0.0 copy-done.3
  16.0 0.6 gather_fusion.1
  16.6 0.6 pad_clamp_fusion
  17.2 0.0 all-to-all-done
  17.2 0.4 reduce
  17.6 6.0 %pick_blocks.1 = bf16[16,128,1536]{2,1,0:T(8,128)(2,1)} custom-call(s32[16]{0:T(128)S(1)} %and_select_fusion.ids_ref, bf16[1024,2048]{1,0:T(8,128)(2,1)} %stored_ref.3), custom_call_target="tpu_custom_call" | custom-call | bytes 12582912 | tf_op jit(solution)/shard_map/pick_blocks/pallas_call | solution.py:65
  23.7 0.0 copy-done.10
  23.7 4.6 %all-to-all-start.1 = ((bf16[16,128,1536]{2,1,0:T(8,128)(2,1)}), bf16[16,128,1536]{2,1,0:T(8,128)(2,1)}, u32[]{:S(2)}, u32[]{:S(2)}) async-start(bf16[16,128,1536]{2,1,0:T(8,128)(2,1)} %pick_blocks.1), calls=%async_computation.1 | async-start | bytes 12582912 | tf_op jit(solution)/shard_map/all_to_all | solution.py:331
  28.3 29.6 %collective-permute-done.1.refs_1_ = bf16[1024,384]{1,0:T(8,128)(2,1)S(1)} collective-permute-done((bf16[1024,384]{1,0:T(8,128)(2,1)S(1)}, bf16[1024,384]{1,0:T(8,128)(2,1)S(1)}, u32[]{:S(2)}, u32[]{:S(2)}) %collective-permute-start.1) | collective-permute-done | bytes 786464 | tf_op jit(solution)/shard_map/ppermute | solution.py:341
  57.9 0.6 gather_fusion.2
  58.6 0.1 copy.27.ids_ref
  58.7 0.1 copy-done.9
  58.8 2.4 %pick_pairs.1 = bf16[8,2,128,512]{3,2,1,0:T(8,128)(2,1)S(1)} custom-call(s32[8,2]{1,0:T(8,128)S(1)} %copy.27.ids_ref, bf16[1024,2048]{1,0:T(8,128)(2,1)} %stored_ref.3, bf16[1024,128]{1,0:T(8,128)(2,1)} %copy-done.10, bf16[1024,384]{1,0:T(8,128)(2,1)} %copy-done.9), custom_call_target="tpu_custom_call" | custom-call | flops 999999995904 | bytes 1000000000 | tf_op jit(solution)/shard_map/pick_pairs/pallas_call | solution.py:110
  61.3 0.0 copy-start.1
  61.3 1.3 copy-done.1
  62.6 0.0 copy-start.7
  62.6 0.0 copy-start.4
  62.6 0.0 copy-start.8
  62.6 1.0 slice_bitcast_fusion
  63.6 0.0 collective-permute-start.2
  63.6 0.0 copy-done.7
  63.6 0.0 copy-done.4
  63.6 0.0 copy-done.8
  63.7 0.7 gather_fusion
  64.3 0.1 reshape.170.slots_ref
  64.4 0.0 collective-permute-start.4
  64.4 1.6 collective-permute-start.3
  66.0 1.0 fusion
  67.0 1.7 collective-permute-start.8
  68.6 1.9 collective-permute-start.7
  70.5 10.0 %collective-permute-done.2 = bf16[2,128,512]{2,1,0:T(8,128)(2,1)} collective-permute-done((bf16[2,128,512]{2,1,0:T(8,128)(2,1)}, bf16[2,128,512]{2,1,0:T(8,128)(2,1)}, u32[]{:S(2)}, u32[]{:S(2)}) %collective-permute-start.2) | collective-permute-done | bytes 262176 | tf_op jit(solution)/shard_map/ppermute | solution.py:354
  80.5 0.0 collective-permute-start.5
  80.5 1.0 constant_dynamic-update-slice_fusion.6
  81.5 59.7 %collective-permute-done.3 = bf16[2,128,512]{2,1,0:T(8,128)(2,1)S(1)} collective-permute-done((bf16[2,128,512]{2,1,0:T(8,128)(2,1)}, bf16[2,128,512]{2,1,0:T(8,128)(2,1)S(1)}, u32[]{:S(2)}, u32[]{:S(2)}) %collective-permute-start.3) | collective-permute-done | bytes 262176 | tf_op jit(solution)/shard_map/ppermute | solution.py:354
  141.2 0.0 collective-permute-start.6
  141.3 0.0 collective-permute-done.4
  141.3 0.0 collective-permute-done.5
  141.3 9.3 %collective-permute-done.6 = bf16[2,128,512]{2,1,0:T(8,128)(2,1)S(1)} collective-permute-done((bf16[2,128,512]{2,1,0:T(8,128)(2,1)S(1)}, bf16[2,128,512]{2,1,0:T(8,128)(2,1)S(1)}, u32[]{:S(2)}, u32[]{:S(2)}) %collective-permute-start.6) | collective-permute-done | bytes 262176 | tf_op jit(solution)/shard_map/ppermute | solution.py:354
  150.7 0.0 collective-permute-done.7
  150.7 0.0 collective-permute-done.8
  150.7 0.0 copy-start.5
  150.7 1.3 copy-done.5
  152.0 0.0 copy-done
  152.1 3.0 %near_scores.1.before_ref = f32[4,128,512]{2,1,0:T(8,128)S(1)} custom-call(s32[4,4]{1,0:T(4,128)S(1)} %fusion.5.near_slots_ref, bf16[512,2048]{1,0:T(8,128)(2,1)S(1)} %copy-done, bf16[16,128,512]{2,1,0:T(8,128)(2,1)} %copy-done.5), custom_call_target="tpu_custom_call" | custom-call | flops 268435456 | bytes 4194304 | tf_op jit(solution)/shard_map/near_scores/pallas_call | solution.py:165
  155.1 32.1 %all-to-all-done.1.fetched_ref = bf16[16,128,1536]{2,1,0:T(8,128)(2,1)} async-done(((bf16[16,128,1536]{2,1,0:T(8,128)(2,1)}), bf16[16,128,1536]{2,1,0:T(8,128)(2,1)}, u32[]{:S(2)}, u32[]{:S(2)}) %all-to-all-start.1) | async-done | bytes 6291488 | tf_op jit(solution)/shard_map/all_to_all | solution.py:331
  187.2 0.0 copy-done.2
  187.2 4.9 %partial_scores.1 = (f32[4,128,512]{2,1,0:T(8,128)S(1)}, bf16[16,128,2048]{2,1,0:T(8,128)(2,1)S(1)}, s32[4,1,128]{2,1,0:T(1,128)S(1)}) custom-call(s32[4,4]{1,0:T(4,128)S(1)} %fusion.5.near_slots_ref, s32[4,4]{1,0:T(4,128)S(1)} %reshape.170.slots_ref, bf16[512,2048]{1,0:T(8,128)(2,1)S(1)} %copy-done, s32[4,1,128]{2,1,0:T(1,128)S(1)} %bitcast.43, ...), custom_call_target="tpu_custom_call" | custom-call | flops 805306368 | bytes 10485760 | tf_op jit(solution)/shard_map/partial_scores/pallas_call | solution.py:216
  192.1 0.5 collective-permute-start.9
  192.6 2.3 %collective-permute-done.9.refs_1_ = f32[4,128,512]{2,1,0:T(8,128)S(1)} collective-permute-done((f32[4,128,512]{2,1,0:T(8,128)S(1)}, f32[4,128,512]{2,1,0:T(8,128)S(1)}, u32[]{:S(2)}, u32[]{:S(2)}) %collective-permute-start.9) | collective-permute-done | bytes 1048608 | tf_op jit(solution)/shard_map/ppermute | solution.py:372
  194.9 4.2 %losses_and_gradients.1 = (f32[2,1,128]{2,1,0:T(1,128)}, bf16[512,2048]{1,0:T(8,128)(2,1)}) custom-call(s32[1]{0:T(128)} %bitcast.share_ref, f32[4,128,512]{2,1,0:T(8,128)S(1)} %get-tuple-element.19.refs_0_, f32[4,128,512]{2,1,0:T(8,128)S(1)} %collective-permute-done.9.refs_1_, bf16[16,128,2048]{2,1,0:T(8,128)(2,1)S(1)} %get-tuple-element.20.refs_2_, ...), custom_call_target="tpu_custom_call" | custom-call | flops 1073741824 | bytes 2097152 | tf_op jit(solution)/shard_map/losses_and_gradients/pallas_call | solution.py:283
  (16 shorter events, 0.2 us)
Async XLA Ops:
  0.6 15.3 %copy-start.3 = (s32[16]{0:T(128)S(1)}, s32[16]{0:T(128)}, u32[]{:S(2)}) copy-start(s32[16]{0:T(128)} %constant.117.clone) | copy-start | bytes 196
  1.6 13.1 %collective-permute-start = (bf16[1024,128]{1,0:T(8,128)(2,1)S(1)}, bf16[1024,128]{1,0:T(8,128)(2,1)S(1)}, u32[]{:S(2)}, u32[]{:S(2)}) collective-permute-start(bf16[1024,128]{1,0:T(8,128)(2,1)S(1)} %slice.31), channel_id=1, source_target_pairs={{0,24},{2,26},{4,28},{6,30},{8,16},{10,18},{12,20},{14,22},{16,8},... | collective-permute-start | bytes 786440 | tf_op jit(solution)/shard_map/ppermute | solution.py:324
  3.7 1.5 copy-start.6
  5.1 12.1 %all-to-all-start = ((s32[16,1,1]{2,1,0:T(1,128)}), s32[16,1,1]{2,1,0:T(1,128)S(1)}, u32[]{:S(2)}, u32[]{:S(2)}) async-start(s32[16,1,1]{2,1,0:T(1,128)} %copy.26), calls=%async_computation | async-start | bytes 16384 | tf_op jit(solution)/shard_map/all_to_all | solution.py:331
  14.7 9.0 %copy-start.10 = (bf16[1024,128]{1,0:T(8,128)(2,1)}, bf16[1024,128]{1,0:T(8,128)(2,1)S(1)}, u32[]{:S(2)}) copy-start(bf16[1024,128]{1,0:T(8,128)(2,1)S(1)} %collective-permute-done.refs_0_) | copy-start | bytes 786436
  14.7 43.2 %collective-permute-start.1 = (bf16[1024,384]{1,0:T(8,128)(2,1)S(1)}, bf16[1024,384]{1,0:T(8,128)(2,1)S(1)}, u32[]{:S(2)}, u32[]{:S(2)}) collective-permute-start(bf16[1024,384]{1,0:T(8,128)(2,1)S(1)} %slice.30), channel_id=1, source_target_pairs={{0,24},{2,26},{4,28},{6,30},{8,16},{10,18},{12,20},{14,22},{16,8},... | collective-permute-start | bytes 2359304 | tf_op jit(solution)/shard_map/ppermute | solution.py:341
  23.7 163.5 %all-to-all-start.1 = ((bf16[16,128,1536]{2,1,0:T(8,128)(2,1)}), bf16[16,128,1536]{2,1,0:T(8,128)(2,1)}, u32[]{:S(2)}, u32[]{:S(2)}) async-start(bf16[16,128,1536]{2,1,0:T(8,128)(2,1)} %pick_blocks.1), calls=%async_computation.1 | async-start | bytes 12582912 | tf_op jit(solution)/shard_map/all_to_all | solution.py:331
  57.9 0.9 copy-start.9
  61.3 1.3 copy-start.1
  62.6 1.0 copy-start.7
  62.6 1.1 copy-start.4
  62.6 1.1 copy-start.8
  63.6 16.9 %collective-permute-start.2 = (bf16[2,128,512]{2,1,0:T(8,128)(2,1)}, bf16[2,128,512]{2,1,0:T(8,128)(2,1)}, u32[]{:S(2)}, u32[]{:S(2)}) collective-permute-start(bf16[2,128,512]{2,1,0:T(8,128)(2,1)} %get-tuple-element.34), channel_id=1, source_target_pairs={{0,2},{2,4},{4,6},{6,8},{8,10},{10,12},{12,14},{14,0},{16,18},{18,... | collective-permute-start | bytes 786440 | tf_op jit(solution)/shard_map/ppermute | solution.py:354
  64.4 76.9 %collective-permute-start.4 = (bf16[2,128,512]{2,1,0:T(8,128)(2,1)S(1)}, bf16[2,128,512]{2,1,0:T(8,128)(2,1)S(1)}, u32[]{:S(2)}, u32[]{:S(2)}) collective-permute-start(bf16[2,128,512]{2,1,0:T(8,128)(2,1)S(1)} %get-tuple-element.32), channel_id=1, source_target_pairs={{0,6},{2,8},{4,10},{6,12},{8,14},{10,0},{12,2},{14,4},{16,22},{18,... | collective-permute-start | bytes 786440 | tf_op jit(solution)/shard_map/ppermute | solution.py:354
  64.4 87.6 %copy-start = (bf16[512,2048]{1,0:T(8,128)(2,1)S(1)}, bf16[512,2048]{1,0:T(8,128)(2,1)}, u32[]{:S(2)}) copy-start(bf16[512,2048]{1,0:T(8,128)(2,1)} %query_ref.3) | copy-start | bytes 6291460
  64.4 76.8 %collective-permute-start.3 = (bf16[2,128,512]{2,1,0:T(8,128)(2,1)}, bf16[2,128,512]{2,1,0:T(8,128)(2,1)S(1)}, u32[]{:S(2)}, u32[]{:S(2)}) collective-permute-start(bf16[2,128,512]{2,1,0:T(8,128)(2,1)} %get-tuple-element.33), channel_id=1, source_target_pairs={{0,4},{2,6},{4,8},{6,10},{8,12},{10,14},{12,0},{14,2},{16,20},{18,... | collective-permute-start | bytes 786440 | tf_op jit(solution)/shard_map/ppermute | solution.py:354
  67.0 83.7 %collective-permute-start.8 = (bf16[2,128,512]{2,1,0:T(8,128)(2,1)S(1)}, bf16[2,128,512]{2,1,0:T(8,128)(2,1)S(1)}, u32[]{:S(2)}, u32[]{:S(2)}) collective-permute-start(bf16[2,128,512]{2,1,0:T(8,128)(2,1)S(1)} %get-tuple-element.28), channel_id=1, source_target_pairs={{0,14},{2,0},{4,2},{6,4},{8,6},{10,8},{12,10},{14,12},{16,30},{18,... | collective-permute-start | bytes 786440 | tf_op jit(solution)/shard_map/ppermute | solution.py:354
  68.6 82.0 %collective-permute-start.7 = (bf16[2,128,512]{2,1,0:T(8,128)(2,1)S(1)}, bf16[2,128,512]{2,1,0:T(8,128)(2,1)S(1)}, u32[]{:S(2)}, u32[]{:S(2)}) collective-permute-start(bf16[2,128,512]{2,1,0:T(8,128)(2,1)S(1)} %get-tuple-element.29), channel_id=1, source_target_pairs={{0,12},{2,14},{4,0},{6,2},{8,4},{10,6},{12,8},{14,10},{16,28},{18,... | collective-permute-start | bytes 786440 | tf_op jit(solution)/shard_map/ppermute | solution.py:354
  80.5 60.8 %collective-permute-start.5 = (bf16[2,128,512]{2,1,0:T(8,128)(2,1)S(1)}, bf16[2,128,512]{2,1,0:T(8,128)(2,1)S(1)}, u32[]{:S(2)}, u32[]{:S(2)}) collective-permute-start(bf16[2,128,512]{2,1,0:T(8,128)(2,1)S(1)} %get-tuple-element.31), channel_id=1, source_target_pairs={{0,8},{2,10},{4,12},{6,14},{8,0},{10,2},{12,4},{14,6},{16,24},{18,... | collective-permute-start | bytes 786440 | tf_op jit(solution)/shard_map/ppermute | solution.py:354
  141.2 9.4 %collective-permute-start.6 = (bf16[2,128,512]{2,1,0:T(8,128)(2,1)S(1)}, bf16[2,128,512]{2,1,0:T(8,128)(2,1)S(1)}, u32[]{:S(2)}, u32[]{:S(2)}) collective-permute-start(bf16[2,128,512]{2,1,0:T(8,128)(2,1)S(1)} %get-tuple-element.30), channel_id=1, source_target_pairs={{0,10},{2,12},{4,14},{6,0},{8,2},{10,4},{12,6},{14,8},{16,26},{18,... | collective-permute-start | bytes 786440 | tf_op jit(solution)/shard_map/ppermute | solution.py:354
  150.7 1.3 copy-start.5
  152.1 35.1 %copy-start.2 = (s32[512]{0:T(512)S(1)}, s32[512]{0:T(512)}, u32[]{:S(2)}) copy-start(s32[512]{0:T(512)} %param.9) | copy-start | bytes 6148
  192.1 2.8 %collective-permute-start.9 = (f32[4,128,512]{2,1,0:T(8,128)S(1)}, f32[4,128,512]{2,1,0:T(8,128)S(1)}, u32[]{:S(2)}, u32[]{:S(2)}) collective-permute-start(f32[4,128,512]{2,1,0:T(8,128)S(1)} %get-tuple-element.19.refs_0_), channel_id=1, source_target_pairs={{0,1},{1,0},{2,3},{3,2},{4,5},{5,4},{6,7},{7,6},{8,9},{9,8},{10,11... | collective-permute-start | bytes 3145736 | tf_op jit(solution)/shard_map/ppermute | solution.py:372

commit v6 on v5

--- a/solution.py
+++ b/solution.py
@@ -114,7 +114,7 @@
         out_specs=IN_VMEM,
         scratch_shapes=[pltpu.SemaphoreType.DMA((count * (1 + len(far_parts)),))],
         compiler_params=pltpu.CompilerParams(vmem_limit_bytes=VMEM_LIMIT),
-        cost_estimate=pl.CostEstimate(flops=10**12, bytes_accessed=10**9, transcendentals=0),
+        cost_estimate=pl.CostEstimate(flops=10**11, bytes_accessed=10**9, transcendentals=0),
         name="pick_pairs",
     )(ids, hbm(passage_emb), *[hbm(part) for part in far_parts])
 
@@ -324,7 +324,8 @@
     early_half = lax.ppermute(passage_emb[:, :first], "dp", to_other_half)
 
     quarter = dp_count // 4
-    order = [quarter * z + c for c in range(quarter) for z in (0, 3, 1, 2)]
+    columns = [*range(0, quarter, 2), *range(1, quarter, 2)]
+    order = [quarter * z + c for c in columns for z in (0, 3, 1, 2)]
     places = jnp.asarray([order.index(d) for d in range(dp_count)], jnp.int32)
 
     def all_to_all(array):

time: 203 us -> 202 us (level); the launches traced: 199 us -> 201 us
    all_to_all x2, waiting for transfers between devices: 32.1 us -> 35.9 us  [all_to_all(): lax.all_to_all(array, 'dp', split_axis=0, concat_axis=0, tiled=True, axis...]
    unnamed x29 -> x21, local copies, waits for them, and re-layouts: 4.81 us -> 4.93 us
  transfers between devices with their start and end apart: 12 -> 12, of which waited for: 7 -> 8; matrix products, arithmetic and copies ran while one was open for 5% -> 5% of each run, Pallas kernels for 6% -> 6%
where the time goes in v6:
time: 202 us; the launch traced here: 201 us
  waiting for transfers between devices  148 us (73%)
  Pallas kernels  20.5 us (10%)
  starting transfers between devices  18.6 us (9%)
  local copies, waits for them, and re-layouts  11 us (5%)
    ppermute x7, waiting for transfers between devices, shards(): lax.ppermute(pairs[k], 'dp', [(d, d - d % half + (d % half + k) % half) f...  78.5 us
    all_to_all x2, waiting for transfers between devices, all_to_all(): lax.all_to_all(array, 'dp', split_axis=0, concat_axis=0, tiled=True, axis...  35.9 us
    ppermute x1, waiting for transfers between devices, shards(): far_parts = [early_half, lax.ppermute(late_half, 'dp', to_other_half)]  28.3 us
    all_to_all x2, starting transfers between devices, all_to_all(): lax.all_to_all(array, 'dp', split_axis=0, concat_axis=0, tiled=True, axis...  11.7 us
    pallas_call x1, Pallas kernels, pick_blocks(): pl.pallas_call(pick_kernel, out_shape=pltpu.HBM((count, block_rows, featu...  6.01 us
    unnamed x21, local copies, waits for them, and re-layouts  4.93 us
    pallas_call x1, Pallas kernels, partial_scores(): pl.pallas_call(score_kernel, out_shape=(pltpu.VMEM((query_blocks, block_r...  4.91 us
    pallas_call x1, Pallas kernels, losses_and_gradients(): pl.pallas_call(functools.partial(gradient_kernel, len(scores)), out_shape...  4.15 us
  transfers between devices with their start and end apart: 12, of which 8 were waited for; matrix products, arithmetic and copies ran while one was open for 5% of the time, Pallas kernels for 6%

profile of v6, /device:TPU:11, one launch (start us, length us, event | category | flops | bytes accessed | tf_op | source)
XLA Modules:
  0.0 200.7 jit_solution(15631349782535837548)
XLA Ops:
  0.6 1.0 slice.31
  1.6 1.4 collective-permute-start
  3.0 0.7 broadcast_multiply_fusion
  3.7 0.8 add_reduce_fusion
  4.4 0.7 copy.26
  5.1 5.6 %all-to-all-start = ((s32[16,1,1]{2,1,0:T(1,128)}), s32[16,1,1]{2,1,0:T(1,128)S(1)}, u32[]{:S(2)}, u32[]{:S(2)}) async-start(s32[16,1,1]{2,1,0:T(1,128)} %copy.26), calls=%async_computation | async-start | bytes 16384 | tf_op jit(solution)/shard_map/all_to_all | solution.py:332
  10.7 1.2 slice.30
  11.9 2.7 %collective-permute-done.refs_0_ = bf16[1024,128]{1,0:T(8,128)(2,1)S(1)} collective-permute-done((bf16[1024,128]{1,0:T(8,128)(2,1)S(1)}, bf16[1024,128]{1,0:T(8,128)(2,1)S(1)}, u32[]{:S(2)}, u32[]{:S(2)}) %collective-permute-start) | collective-permute-done | bytes 262176 | tf_op jit(solution)/shard_map/ppermute | solution.py:324
  14.7 0.0 copy-start.6
  14.7 1.2 collective-permute-start.1
  15.8 0.0 all-to-all-done
  15.8 0.4 reduce
  16.2 6.0 %pick_blocks.1 = bf16[16,128,1536]{2,1,0:T(8,128)(2,1)} custom-call(s32[16]{0:T(128)S(1)} %and_select_fusion.ids_ref, bf16[1024,2048]{1,0:T(8,128)(2,1)} %stored_ref.3), custom_call_target="tpu_custom_call" | custom-call | bytes 12582912 | tf_op jit(solution)/shard_map/pick_blocks/pallas_call | solution.py:65
  22.3 0.0 copy-done.6
  22.3 0.0 copy-start.3
  22.3 6.0 %all-to-all-start.1 = ((bf16[16,128,1536]{2,1,0:T(8,128)(2,1)}), bf16[16,128,1536]{2,1,0:T(8,128)(2,1)}, u32[]{:S(2)}, u32[]{:S(2)}) async-start(bf16[16,128,1536]{2,1,0:T(8,128)(2,1)} %pick_blocks.1), calls=%async_computation.1 | async-start | bytes 12582912 | tf_op jit(solution)/shard_map/all_to_all | solution.py:332
  28.3 0.1 reshape.171
  28.4 0.0 copy-done.3
  28.4 0.6 gather_fusion.1
  29.1 28.3 %collective-permute-done.1.refs_1_ = bf16[1024,384]{1,0:T(8,128)(2,1)S(1)} collective-permute-done((bf16[1024,384]{1,0:T(8,128)(2,1)S(1)}, bf16[1024,384]{1,0:T(8,128)(2,1)S(1)}, u32[]{:S(2)}, u32[]{:S(2)}) %collective-permute-start.1) | collective-permute-done | bytes 786464 | tf_op jit(solution)/shard_map/ppermute | solution.py:342
  57.4 0.0 copy-start.5
  57.4 0.6 gather_fusion.2
  58.0 0.1 copy.27.ids_ref
  58.1 0.1 copy-done.5
  58.2 2.4 %pick_pairs.1 = bf16[8,2,128,512]{3,2,1,0:T(8,128)(2,1)S(1)} custom-call(s32[8,2]{1,0:T(8,128)S(1)} %copy.27.ids_ref, bf16[1024,2048]{1,0:T(8,128)(2,1)} %stored_ref.3, bf16[1024,128]{1,0:T(8,128)(2,1)} %copy-done.6, bf16[1024,384]{1,0:T(8,128)(2,1)} %copy-done.5), custom_call_target="tpu_custom_call" | custom-call | flops 99999997952 | bytes 1000000000 | tf_op jit(solution)/shard_map/pick_pairs/pallas_call | solution.py:110
  60.7 0.0 copy-start.1
  60.7 1.3 copy-done.1
  62.0 1.0 slice_bitcast_fusion
  63.0 0.0 collective-permute-start.2
  63.1 0.7 gather_fusion
  63.7 0.1 reshape.170.slots_ref
  63.8 0.0 collective-permute-start.4
  63.8 0.0 copy-start
  63.8 0.1 collective-permute-start.3
  63.9 1.1 fusion
  65.0 1.5 collective-permute-start.8
  66.5 2.4 %collective-permute-start.7 = (bf16[2,128,512]{2,1,0:T(8,128)(2,1)S(1)}, bf16[2,128,512]{2,1,0:T(8,128)(2,1)S(1)}, u32[]{:S(2)}, u32[]{:S(2)}) collective-permute-start(bf16[2,128,512]{2,1,0:T(8,128)(2,1)S(1)} %get-tuple-element.29), channel_id=1, source_target_pairs={{0,12},{2,14},{4,0},{6,2},{8,4},{10,6},{12,8},{14,10},{16,28},{18,... | collective-permute-start | bytes 786440 | tf_op jit(solution)/shard_map/ppermute | solution.py:355
  68.9 6.0 %collective-permute-done.2 = bf16[2,128,512]{2,1,0:T(8,128)(2,1)} collective-permute-done((bf16[2,128,512]{2,1,0:T(8,128)(2,1)}, bf16[2,128,512]{2,1,0:T(8,128)(2,1)}, u32[]{:S(2)}, u32[]{:S(2)}) %collective-permute-start.2) | collective-permute-done | bytes 262176 | tf_op jit(solution)/shard_map/ppermute | solution.py:355
  74.9 0.0 collective-permute-start.5
  74.9 1.0 constant_dynamic-update-slice_fusion.6
  75.8 62.5 %collective-permute-done.3 = bf16[2,128,512]{2,1,0:T(8,128)(2,1)S(1)} collective-permute-done((bf16[2,128,512]{2,1,0:T(8,128)(2,1)}, bf16[2,128,512]{2,1,0:T(8,128)(2,1)S(1)}, u32[]{:S(2)}, u32[]{:S(2)}) %collective-permute-start.3) | collective-permute-done | bytes 262176 | tf_op jit(solution)/shard_map/ppermute | solution.py:355
  138.3 0.0 collective-permute-start.6
  138.4 0.0 collective-permute-done.4
  138.4 1.1 collective-permute-done.5
  139.5 8.9 %collective-permute-done.6 = bf16[2,128,512]{2,1,0:T(8,128)(2,1)S(1)} collective-permute-done((bf16[2,128,512]{2,1,0:T(8,128)(2,1)S(1)}, bf16[2,128,512]{2,1,0:T(8,128)(2,1)S(1)}, u32[]{:S(2)}, u32[]{:S(2)}) %collective-permute-start.6) | collective-permute-done | bytes 262176 | tf_op jit(solution)/shard_map/ppermute | solution.py:355
  148.5 0.0 collective-permute-done.7
  148.5 0.0 collective-permute-done.8
  148.5 0.0 copy-start.4
  148.5 1.3 copy-done.4
  149.9 0.0 copy-done
  149.9 0.0 copy-start.2
  149.9 3.0 %near_scores.1.before_ref = f32[4,128,512]{2,1,0:T(8,128)S(1)} custom-call(s32[4,4]{1,0:T(4,128)S(1)} %fusion.5.near_slots_ref, bf16[512,2048]{1,0:T(8,128)(2,1)S(1)} %copy-done, bf16[16,128,512]{2,1,0:T(8,128)(2,1)} %copy-done.4), custom_call_target="tpu_custom_call" | custom-call | flops 268435456 | bytes 4194304 | tf_op jit(solution)/shard_map/near_scores/pallas_call | solution.py:165
  152.9 35.9 %all-to-all-done.1.fetched_ref = bf16[16,128,1536]{2,1,0:T(8,128)(2,1)} async-done(((bf16[16,128,1536]{2,1,0:T(8,128)(2,1)}), bf16[16,128,1536]{2,1,0:T(8,128)(2,1)}, u32[]{:S(2)}, u32[]{:S(2)}) %all-to-all-start.1) | async-done | bytes 6291488 | tf_op jit(solution)/shard_map/all_to_all | solution.py:332
  188.8 0.0 copy-done.2
  188.8 4.9 %partial_scores.1 = (f32[4,128,512]{2,1,0:T(8,128)S(1)}, bf16[16,128,2048]{2,1,0:T(8,128)(2,1)S(1)}, s32[4,1,128]{2,1,0:T(1,128)S(1)}) custom-call(s32[4,4]{1,0:T(4,128)S(1)} %fusion.5.near_slots_ref, s32[4,4]{1,0:T(4,128)S(1)} %reshape.170.slots_ref, bf16[512,2048]{1,0:T(8,128)(2,1)S(1)} %copy-done, s32[4,1,128]{2,1,0:T(1,128)S(1)} %bitcast.43, ...), custom_call_target="tpu_custom_call" | custom-call | flops 805306368 | bytes 10485760 | tf_op jit(solution)/shard_map/partial_scores/pallas_call | solution.py:216
  193.8 0.5 collective-permute-start.9
  194.2 2.3 %collective-permute-done.9.refs_1_ = f32[4,128,512]{2,1,0:T(8,128)S(1)} collective-permute-done((f32[4,128,512]{2,1,0:T(8,128)S(1)}, f32[4,128,512]{2,1,0:T(8,128)S(1)}, u32[]{:S(2)}, u32[]{:S(2)}) %collective-permute-start.9) | collective-permute-done | bytes 1048608 | tf_op jit(solution)/shard_map/ppermute | solution.py:373
  196.5 4.2 %losses_and_gradients.1 = (f32[2,1,128]{2,1,0:T(1,128)}, bf16[512,2048]{1,0:T(8,128)(2,1)}) custom-call(s32[1]{0:T(128)} %bitcast.share_ref, f32[4,128,512]{2,1,0:T(8,128)S(1)} %get-tuple-element.19.refs_0_, f32[4,128,512]{2,1,0:T(8,128)S(1)} %collective-permute-done.9.refs_1_, bf16[16,128,2048]{2,1,0:T(8,128)(2,1)S(1)} %get-tuple-element.20.refs_2_, ...), custom_call_target="tpu_custom_call" | custom-call | flops 1073741824 | bytes 2097152 | tf_op jit(solution)/shard_map/losses_and_gradients/pallas_call | solution.py:283
  (14 shorter events, 0.2 us)
Async XLA Ops:
  1.6 13.1 %collective-permute-start = (bf16[1024,128]{1,0:T(8,128)(2,1)S(1)}, bf16[1024,128]{1,0:T(8,128)(2,1)S(1)}, u32[]{:S(2)}, u32[]{:S(2)}) collective-permute-start(bf16[1024,128]{1,0:T(8,128)(2,1)S(1)} %slice.31), channel_id=1, source_target_pairs={{0,24},{2,26},{4,28},{6,30},{8,16},{10,18},{12,20},{14,22},{16,8},... | collective-permute-start | bytes 786440 | tf_op jit(solution)/shard_map/ppermute | solution.py:324
  5.1 10.7 %all-to-all-start = ((s32[16,1,1]{2,1,0:T(1,128)}), s32[16,1,1]{2,1,0:T(1,128)S(1)}, u32[]{:S(2)}, u32[]{:S(2)}) async-start(s32[16,1,1]{2,1,0:T(1,128)} %copy.26), calls=%async_computation | async-start | bytes 16384 | tf_op jit(solution)/shard_map/all_to_all | solution.py:332
  14.7 7.6 %copy-start.6 = (bf16[1024,128]{1,0:T(8,128)(2,1)}, bf16[1024,128]{1,0:T(8,128)(2,1)S(1)}, u32[]{:S(2)}) copy-start(bf16[1024,128]{1,0:T(8,128)(2,1)S(1)} %collective-permute-done.refs_0_) | copy-start | bytes 786436
  14.7 42.7 %collective-permute-start.1 = (bf16[1024,384]{1,0:T(8,128)(2,1)S(1)}, bf16[1024,384]{1,0:T(8,128)(2,1)S(1)}, u32[]{:S(2)}, u32[]{:S(2)}) collective-permute-start(bf16[1024,384]{1,0:T(8,128)(2,1)S(1)} %slice.30), channel_id=1, source_target_pairs={{0,24},{2,26},{4,28},{6,30},{8,16},{10,18},{12,20},{14,22},{16,8},... | collective-permute-start | bytes 2359304 | tf_op jit(solution)/shard_map/ppermute | solution.py:342
  22.3 6.2 %copy-start.3 = (s32[16]{0:T(128)S(1)}, s32[16]{0:T(128)}, u32[]{:S(2)}) copy-start(s32[16]{0:T(128)} %constant.117.clone) | copy-start | bytes 196
  22.3 166.6 %all-to-all-start.1 = ((bf16[16,128,1536]{2,1,0:T(8,128)(2,1)}), bf16[16,128,1536]{2,1,0:T(8,128)(2,1)}, u32[]{:S(2)}, u32[]{:S(2)}) async-start(bf16[16,128,1536]{2,1,0:T(8,128)(2,1)} %pick_blocks.1), calls=%async_computation.1 | async-start | bytes 12582912 | tf_op jit(solution)/shard_map/all_to_all | solution.py:332
  57.4 0.9 copy-start.5
  60.7 1.3 copy-start.1
  63.0 11.8 %collective-permute-start.2 = (bf16[2,128,512]{2,1,0:T(8,128)(2,1)}, bf16[2,128,512]{2,1,0:T(8,128)(2,1)}, u32[]{:S(2)}, u32[]{:S(2)}) collective-permute-start(bf16[2,128,512]{2,1,0:T(8,128)(2,1)} %get-tuple-element.34), channel_id=1, source_target_pairs={{0,2},{2,4},{4,6},{6,8},{8,10},{10,12},{12,14},{14,0},{16,18},{18,... | collective-permute-start | bytes 786440 | tf_op jit(solution)/shard_map/ppermute | solution.py:355
  63.8 74.6 %collective-permute-start.4 = (bf16[2,128,512]{2,1,0:T(8,128)(2,1)S(1)}, bf16[2,128,512]{2,1,0:T(8,128)(2,1)S(1)}, u32[]{:S(2)}, u32[]{:S(2)}) collective-permute-start(bf16[2,128,512]{2,1,0:T(8,128)(2,1)S(1)} %get-tuple-element.32), channel_id=1, source_target_pairs={{0,6},{2,8},{4,10},{6,12},{8,14},{10,0},{12,2},{14,4},{16,22},{18,... | collective-permute-start | bytes 786440 | tf_op jit(solution)/shard_map/ppermute | solution.py:355
  63.8 86.1 %copy-start = (bf16[512,2048]{1,0:T(8,128)(2,1)S(1)}, bf16[512,2048]{1,0:T(8,128)(2,1)}, u32[]{:S(2)}) copy-start(bf16[512,2048]{1,0:T(8,128)(2,1)} %query_ref.3) | copy-start | bytes 6291460
  63.8 74.5 %collective-permute-start.3 = (bf16[2,128,512]{2,1,0:T(8,128)(2,1)}, bf16[2,128,512]{2,1,0:T(8,128)(2,1)S(1)}, u32[]{:S(2)}, u32[]{:S(2)}) collective-permute-start(bf16[2,128,512]{2,1,0:T(8,128)(2,1)} %get-tuple-element.33), channel_id=1, source_target_pairs={{0,4},{2,6},{4,8},{6,10},{8,12},{10,14},{12,0},{14,2},{16,20},{18,... | collective-permute-start | bytes 786440 | tf_op jit(solution)/shard_map/ppermute | solution.py:355
  65.0 83.5 %collective-permute-start.8 = (bf16[2,128,512]{2,1,0:T(8,128)(2,1)S(1)}, bf16[2,128,512]{2,1,0:T(8,128)(2,1)S(1)}, u32[]{:S(2)}, u32[]{:S(2)}) collective-permute-start(bf16[2,128,512]{2,1,0:T(8,128)(2,1)S(1)} %get-tuple-element.28), channel_id=1, source_target_pairs={{0,14},{2,0},{4,2},{6,4},{8,6},{10,8},{12,10},{14,12},{16,30},{18,... | collective-permute-start | bytes 786440 | tf_op jit(solution)/shard_map/ppermute | solution.py:355
  66.5 82.0 %collective-permute-start.7 = (bf16[2,128,512]{2,1,0:T(8,128)(2,1)S(1)}, bf16[2,128,512]{2,1,0:T(8,128)(2,1)S(1)}, u32[]{:S(2)}, u32[]{:S(2)}) collective-permute-start(bf16[2,128,512]{2,1,0:T(8,128)(2,1)S(1)} %get-tuple-element.29), channel_id=1, source_target_pairs={{0,12},{2,14},{4,0},{6,2},{8,4},{10,6},{12,8},{14,10},{16,28},{18,... | collective-permute-start | bytes 786440 | tf_op jit(solution)/shard_map/ppermute | solution.py:355
  74.9 64.6 %collective-permute-start.5 = (bf16[2,128,512]{2,1,0:T(8,128)(2,1)S(1)}, bf16[2,128,512]{2,1,0:T(8,128)(2,1)S(1)}, u32[]{:S(2)}, u32[]{:S(2)}) collective-permute-start(bf16[2,128,512]{2,1,0:T(8,128)(2,1)S(1)} %get-tuple-element.31), channel_id=1, source_target_pairs={{0,8},{2,10},{4,12},{6,14},{8,0},{10,2},{12,4},{14,6},{16,24},{18,... | collective-permute-start | bytes 786440 | tf_op jit(solution)/shard_map/ppermute | solution.py:355
  138.3 10.1 %collective-permute-start.6 = (bf16[2,128,512]{2,1,0:T(8,128)(2,1)S(1)}, bf16[2,128,512]{2,1,0:T(8,128)(2,1)S(1)}, u32[]{:S(2)}, u32[]{:S(2)}) collective-permute-start(bf16[2,128,512]{2,1,0:T(8,128)(2,1)S(1)} %get-tuple-element.30), channel_id=1, source_target_pairs={{0,10},{2,12},{4,14},{6,0},{8,2},{10,4},{12,6},{14,8},{16,26},{18,... | collective-permute-start | bytes 786440 | tf_op jit(solution)/shard_map/ppermute | solution.py:355
  148.5 1.3 copy-start.4
  149.9 39.0 %copy-start.2 = (s32[512]{0:T(512)S(1)}, s32[512]{0:T(512)}, u32[]{:S(2)}) copy-start(s32[512]{0:T(512)} %param.9) | copy-start | bytes 6148
  193.8 2.8 %collective-permute-start.9 = (f32[4,128,512]{2,1,0:T(8,128)S(1)}, f32[4,128,512]{2,1,0:T(8,128)S(1)}, u32[]{:S(2)}, u32[]{:S(2)}) collective-permute-start(f32[4,128,512]{2,1,0:T(8,128)S(1)} %get-tuple-element.19.refs_0_), channel_id=1, source_target_pairs={{0,1},{1,0},{2,3},{3,2},{4,5},{5,4},{6,7},{7,6},{8,9},{9,8},{10,11... | collective-permute-start | bytes 3145736 | tf_op jit(solution)/shard_map/ppermute | solution.py:373

commit v7 on v6

--- a/solution.py
+++ b/solution.py
@@ -8,7 +8,7 @@
 from jax.sharding import PartitionSpec as P
 
 VMEM_LIMIT = 32 * 1024 * 1024
-TILE = 512
+TILE = 1024
 LANES = 128
 WINDOW = 8
 SHIFT = 1 << 16

time: 202 us -> 202 us (level)
  no operation moved by 1% of the time
where the time goes in v7:
time: 202 us; the launch traced here: 201 us
  waiting for transfers between devices  148 us (73%)
  Pallas kernels  20.6 us (10%)
  starting transfers between devices  18.5 us (9%)
  local copies, waits for them, and re-layouts  11 us (5%)
    ppermute x7, waiting for transfers between devices, shards(): lax.ppermute(pairs[k], 'dp', [(d, d - d % half + (d % half + k) % half) f...  78.6 us
    all_to_all x2, waiting for transfers between devices, all_to_all(): lax.all_to_all(array, 'dp', split_axis=0, concat_axis=0, tiled=True, axis...  35.9 us
    ppermute x1, waiting for transfers between devices, shards(): far_parts = [early_half, lax.ppermute(late_half, 'dp', to_other_half)]  28.2 us
    all_to_all x2, starting transfers between devices, all_to_all(): lax.all_to_all(array, 'dp', split_axis=0, concat_axis=0, tiled=True, axis...  11.6 us
    pallas_call x1, Pallas kernels, pick_blocks(): pl.pallas_call(pick_kernel, out_shape=pltpu.HBM((count, block_rows, featu...  6.04 us
    unnamed x21, local copies, waits for them, and re-layouts  4.93 us
    pallas_call x1, Pallas kernels, partial_scores(): pl.pallas_call(score_kernel, out_shape=(pltpu.VMEM((query_blocks, block_r...  4.91 us
    pallas_call x1, Pallas kernels, losses_and_gradients(): pl.pallas_call(functools.partial(gradient_kernel, len(scores)), out_shape...  4.15 us
  transfers between devices with their start and end apart: 12, of which 8 were waited for; matrix products, arithmetic and copies ran while one was open for 5% of the time, Pallas kernels for 6%

profile of v7, /device:TPU:11, one launch (start us, length us, event | category | flops | bytes accessed | tf_op | source)
XLA Modules:
  0.0 200.7 jit_solution(15631349782535837548)
XLA Ops:
  0.6 1.0 slice.31
  1.6 1.4 collective-permute-start
  3.0 0.7 broadcast_multiply_fusion
  3.7 0.8 add_reduce_fusion
  4.4 0.7 copy.26
  5.1 5.6 %all-to-all-start = ((s32[16,1,1]{2,1,0:T(1,128)}), s32[16,1,1]{2,1,0:T(1,128)S(1)}, u32[]{:S(2)}, u32[]{:S(2)}) async-start(s32[16,1,1]{2,1,0:T(1,128)} %copy.26), calls=%async_computation | async-start | bytes 16384 | tf_op jit(solution)/shard_map/all_to_all | solution.py:332
  10.7 1.2 slice.30
  11.9 2.7 %collective-permute-done.refs_0_ = bf16[1024,128]{1,0:T(8,128)(2,1)S(1)} collective-permute-done((bf16[1024,128]{1,0:T(8,128)(2,1)S(1)}, bf16[1024,128]{1,0:T(8,128)(2,1)S(1)}, u32[]{:S(2)}, u32[]{:S(2)}) %collective-permute-start) | collective-permute-done | bytes 262176 | tf_op jit(solution)/shard_map/ppermute | solution.py:324
  14.7 0.0 copy-start.6
  14.7 1.2 collective-permute-start.1
  15.8 0.0 all-to-all-done
  15.8 0.4 reduce
  16.2 6.0 %pick_blocks.1 = bf16[16,128,1536]{2,1,0:T(8,128)(2,1)} custom-call(s32[16]{0:T(128)S(1)} %and_select_fusion.ids_ref, bf16[1024,2048]{1,0:T(8,128)(2,1)} %stored_ref.3), custom_call_target="tpu_custom_call" | custom-call | bytes 12582912 | tf_op jit(solution)/shard_map/pick_blocks/pallas_call | solution.py:65
  22.3 0.0 copy-done.6
  22.3 0.0 copy-start.3
  22.3 6.0 %all-to-all-start.1 = ((bf16[16,128,1536]{2,1,0:T(8,128)(2,1)}), bf16[16,128,1536]{2,1,0:T(8,128)(2,1)}, u32[]{:S(2)}, u32[]{:S(2)}) async-start(bf16[16,128,1536]{2,1,0:T(8,128)(2,1)} %pick_blocks.1), calls=%async_computation.1 | async-start | bytes 12582912 | tf_op jit(solution)/shard_map/all_to_all | solution.py:332
  28.3 0.1 reshape.171
  28.4 0.0 copy-done.3
  28.4 0.6 gather_fusion.1
  29.1 28.2 %collective-permute-done.1.refs_1_ = bf16[1024,384]{1,0:T(8,128)(2,1)S(1)} collective-permute-done((bf16[1024,384]{1,0:T(8,128)(2,1)S(1)}, bf16[1024,384]{1,0:T(8,128)(2,1)S(1)}, u32[]{:S(2)}, u32[]{:S(2)}) %collective-permute-start.1) | collective-permute-done | bytes 786464 | tf_op jit(solution)/shard_map/ppermute | solution.py:342
  57.3 0.0 copy-start.5
  57.3 0.6 gather_fusion.2
  57.9 0.1 copy.27.ids_ref
  58.0 0.1 copy-done.5
  58.1 2.5 %pick_pairs.1 = bf16[8,2,128,512]{3,2,1,0:T(8,128)(2,1)S(1)} custom-call(s32[8,2]{1,0:T(8,128)S(1)} %copy.27.ids_ref, bf16[1024,2048]{1,0:T(8,128)(2,1)} %stored_ref.3, bf16[1024,128]{1,0:T(8,128)(2,1)} %copy-done.6, bf16[1024,384]{1,0:T(8,128)(2,1)} %copy-done.5), custom_call_target="tpu_custom_call" | custom-call | flops 99999997952 | bytes 1000000000 | tf_op jit(solution)/shard_map/pick_pairs/pallas_call | solution.py:110
  60.6 0.0 copy-start.1
  60.7 1.3 copy-done.1
  62.0 1.0 slice_bitcast_fusion
  63.0 0.0 collective-permute-start.2
  63.0 0.7 gather_fusion
  63.7 0.1 reshape.170.slots_ref
  63.8 0.0 collective-permute-start.4
  63.8 0.0 copy-start
  63.8 0.1 collective-permute-start.3
  63.8 1.1 fusion
  64.9 1.5 collective-permute-start.8
  66.5 2.4 %collective-permute-start.7 = (bf16[2,128,512]{2,1,0:T(8,128)(2,1)S(1)}, bf16[2,128,512]{2,1,0:T(8,128)(2,1)S(1)}, u32[]{:S(2)}, u32[]{:S(2)}) collective-permute-start(bf16[2,128,512]{2,1,0:T(8,128)(2,1)S(1)} %get-tuple-element.29), channel_id=1, source_target_pairs={{0,12},{2,14},{4,0},{6,2},{8,4},{10,6},{12,8},{14,10},{16,28},{18,... | collective-permute-start | bytes 786440 | tf_op jit(solution)/shard_map/ppermute | solution.py:355
  68.8 6.0 %collective-permute-done.2 = bf16[2,128,512]{2,1,0:T(8,128)(2,1)} collective-permute-done((bf16[2,128,512]{2,1,0:T(8,128)(2,1)}, bf16[2,128,512]{2,1,0:T(8,128)(2,1)}, u32[]{:S(2)}, u32[]{:S(2)}) %collective-permute-start.2) | collective-permute-done | bytes 262176 | tf_op jit(solution)/shard_map/ppermute | solution.py:355
  74.8 0.0 collective-permute-start.5
  74.8 1.0 constant_dynamic-update-slice_fusion.6
  75.8 62.5 %collective-permute-done.3 = bf16[2,128,512]{2,1,0:T(8,128)(2,1)S(1)} collective-permute-done((bf16[2,128,512]{2,1,0:T(8,128)(2,1)}, bf16[2,128,512]{2,1,0:T(8,128)(2,1)S(1)}, u32[]{:S(2)}, u32[]{:S(2)}) %collective-permute-start.3) | collective-permute-done | bytes 262176 | tf_op jit(solution)/shard_map/ppermute | solution.py:355
  138.3 0.0 collective-permute-start.6
  138.4 0.0 collective-permute-done.4
  138.4 1.1 collective-permute-done.5
  139.5 9.0 %collective-permute-done.6 = bf16[2,128,512]{2,1,0:T(8,128)(2,1)S(1)} collective-permute-done((bf16[2,128,512]{2,1,0:T(8,128)(2,1)S(1)}, bf16[2,128,512]{2,1,0:T(8,128)(2,1)S(1)}, u32[]{:S(2)}, u32[]{:S(2)}) %collective-permute-start.6) | collective-permute-done | bytes 262176 | tf_op jit(solution)/shard_map/ppermute | solution.py:355
  148.5 0.0 collective-permute-done.7
  148.5 0.0 collective-permute-done.8
  148.6 0.0 copy-start.4
  148.6 1.3 copy-done.4
  149.9 0.0 copy-done
  149.9 0.0 copy-start.2
  149.9 3.0 %near_scores.1.before_ref = f32[4,128,512]{2,1,0:T(8,128)S(1)} custom-call(s32[4,4]{1,0:T(4,128)S(1)} %fusion.5.near_slots_ref, bf16[512,2048]{1,0:T(8,128)(2,1)S(1)} %copy-done, bf16[16,128,512]{2,1,0:T(8,128)(2,1)} %copy-done.4), custom_call_target="tpu_custom_call" | custom-call | flops 268435456 | bytes 4194304 | tf_op jit(solution)/shard_map/near_scores/pallas_call | solution.py:165
  152.9 35.9 %all-to-all-done.1.fetched_ref = bf16[16,128,1536]{2,1,0:T(8,128)(2,1)} async-done(((bf16[16,128,1536]{2,1,0:T(8,128)(2,1)}), bf16[16,128,1536]{2,1,0:T(8,128)(2,1)}, u32[]{:S(2)}, u32[]{:S(2)}) %all-to-all-start.1) | async-done | bytes 6291488 | tf_op jit(solution)/shard_map/all_to_all | solution.py:332
  188.9 0.0 copy-done.2
  188.9 4.9 %partial_scores.1 = (f32[4,128,512]{2,1,0:T(8,128)S(1)}, bf16[16,128,2048]{2,1,0:T(8,128)(2,1)S(1)}, s32[4,1,128]{2,1,0:T(1,128)S(1)}) custom-call(s32[4,4]{1,0:T(4,128)S(1)} %fusion.5.near_slots_ref, s32[4,4]{1,0:T(4,128)S(1)} %reshape.170.slots_ref, bf16[512,2048]{1,0:T(8,128)(2,1)S(1)} %copy-done, s32[4,1,128]{2,1,0:T(1,128)S(1)} %bitcast.43, ...), custom_call_target="tpu_custom_call" | custom-call | flops 805306368 | bytes 10485760 | tf_op jit(solution)/shard_map/partial_scores/pallas_call | solution.py:216
  193.8 0.5 collective-permute-start.9
  194.3 2.3 %collective-permute-done.9.refs_1_ = f32[4,128,512]{2,1,0:T(8,128)S(1)} collective-permute-done((f32[4,128,512]{2,1,0:T(8,128)S(1)}, f32[4,128,512]{2,1,0:T(8,128)S(1)}, u32[]{:S(2)}, u32[]{:S(2)}) %collective-permute-start.9) | collective-permute-done | bytes 1048608 | tf_op jit(solution)/shard_map/ppermute | solution.py:373
  196.6 4.2 %losses_and_gradients.1 = (f32[2,1,128]{2,1,0:T(1,128)}, bf16[512,2048]{1,0:T(8,128)(2,1)}) custom-call(s32[1]{0:T(128)} %bitcast.share_ref, f32[4,128,512]{2,1,0:T(8,128)S(1)} %get-tuple-element.19.refs_0_, f32[4,128,512]{2,1,0:T(8,128)S(1)} %collective-permute-done.9.refs_1_, bf16[16,128,2048]{2,1,0:T(8,128)(2,1)S(1)} %get-tuple-element.20.refs_2_, ...), custom_call_target="tpu_custom_call" | custom-call | flops 1073741824 | bytes 2097152 | tf_op jit(solution)/shard_map/losses_and_gradients/pallas_call | solution.py:283
  (14 shorter events, 0.2 us)
Async XLA Ops:
  1.6 13.1 %collective-permute-start = (bf16[1024,128]{1,0:T(8,128)(2,1)S(1)}, bf16[1024,128]{1,0:T(8,128)(2,1)S(1)}, u32[]{:S(2)}, u32[]{:S(2)}) collective-permute-start(bf16[1024,128]{1,0:T(8,128)(2,1)S(1)} %slice.31), channel_id=1, source_target_pairs={{0,24},{2,26},{4,28},{6,30},{8,16},{10,18},{12,20},{14,22},{16,8},... | collective-permute-start | bytes 786440 | tf_op jit(solution)/shard_map/ppermute | solution.py:324
  5.1 10.7 %all-to-all-start = ((s32[16,1,1]{2,1,0:T(1,128)}), s32[16,1,1]{2,1,0:T(1,128)S(1)}, u32[]{:S(2)}, u32[]{:S(2)}) async-start(s32[16,1,1]{2,1,0:T(1,128)} %copy.26), calls=%async_computation | async-start | bytes 16384 | tf_op jit(solution)/shard_map/all_to_all | solution.py:332
  14.7 7.6 %copy-start.6 = (bf16[1024,128]{1,0:T(8,128)(2,1)}, bf16[1024,128]{1,0:T(8,128)(2,1)S(1)}, u32[]{:S(2)}) copy-start(bf16[1024,128]{1,0:T(8,128)(2,1)S(1)} %collective-permute-done.refs_0_) | copy-start | bytes 786436
  14.7 42.6 %collective-permute-start.1 = (bf16[1024,384]{1,0:T(8,128)(2,1)S(1)}, bf16[1024,384]{1,0:T(8,128)(2,1)S(1)}, u32[]{:S(2)}, u32[]{:S(2)}) collective-permute-start(bf16[1024,384]{1,0:T(8,128)(2,1)S(1)} %slice.30), channel_id=1, source_target_pairs={{0,24},{2,26},{4,28},{6,30},{8,16},{10,18},{12,20},{14,22},{16,8},... | collective-permute-start | bytes 2359304 | tf_op jit(solution)/shard_map/ppermute | solution.py:342
  22.3 6.1 %copy-start.3 = (s32[16]{0:T(128)S(1)}, s32[16]{0:T(128)}, u32[]{:S(2)}) copy-start(s32[16]{0:T(128)} %constant.117.clone) | copy-start | bytes 196
  22.3 166.6 %all-to-all-start.1 = ((bf16[16,128,1536]{2,1,0:T(8,128)(2,1)}), bf16[16,128,1536]{2,1,0:T(8,128)(2,1)}, u32[]{:S(2)}, u32[]{:S(2)}) async-start(bf16[16,128,1536]{2,1,0:T(8,128)(2,1)} %pick_blocks.1), calls=%async_computation.1 | async-start | bytes 12582912 | tf_op jit(solution)/shard_map/all_to_all | solution.py:332
  57.3 0.9 copy-start.5
  60.6 1.3 copy-start.1
  63.0 11.8 %collective-permute-start.2 = (bf16[2,128,512]{2,1,0:T(8,128)(2,1)}, bf16[2,128,512]{2,1,0:T(8,128)(2,1)}, u32[]{:S(2)}, u32[]{:S(2)}) collective-permute-start(bf16[2,128,512]{2,1,0:T(8,128)(2,1)} %get-tuple-element.34), channel_id=1, source_target_pairs={{0,2},{2,4},{4,6},{6,8},{8,10},{10,12},{12,14},{14,0},{16,18},{18,... | collective-permute-start | bytes 786440 | tf_op jit(solution)/shard_map/ppermute | solution.py:355
  63.8 74.6 %collective-permute-start.4 = (bf16[2,128,512]{2,1,0:T(8,128)(2,1)S(1)}, bf16[2,128,512]{2,1,0:T(8,128)(2,1)S(1)}, u32[]{:S(2)}, u32[]{:S(2)}) collective-permute-start(bf16[2,128,512]{2,1,0:T(8,128)(2,1)S(1)} %get-tuple-element.32), channel_id=1, source_target_pairs={{0,6},{2,8},{4,10},{6,12},{8,14},{10,0},{12,2},{14,4},{16,22},{18,... | collective-permute-start | bytes 786440 | tf_op jit(solution)/shard_map/ppermute | solution.py:355
  63.8 86.1 %copy-start = (bf16[512,2048]{1,0:T(8,128)(2,1)S(1)}, bf16[512,2048]{1,0:T(8,128)(2,1)}, u32[]{:S(2)}) copy-start(bf16[512,2048]{1,0:T(8,128)(2,1)} %query_ref.3) | copy-start | bytes 6291460
  63.8 74.6 %collective-permute-start.3 = (bf16[2,128,512]{2,1,0:T(8,128)(2,1)}, bf16[2,128,512]{2,1,0:T(8,128)(2,1)S(1)}, u32[]{:S(2)}, u32[]{:S(2)}) collective-permute-start(bf16[2,128,512]{2,1,0:T(8,128)(2,1)} %get-tuple-element.33), channel_id=1, source_target_pairs={{0,4},{2,6},{4,8},{6,10},{8,12},{10,14},{12,0},{14,2},{16,20},{18,... | collective-permute-start | bytes 786440 | tf_op jit(solution)/shard_map/ppermute | solution.py:355
  64.9 83.6 %collective-permute-start.8 = (bf16[2,128,512]{2,1,0:T(8,128)(2,1)S(1)}, bf16[2,128,512]{2,1,0:T(8,128)(2,1)S(1)}, u32[]{:S(2)}, u32[]{:S(2)}) collective-permute-start(bf16[2,128,512]{2,1,0:T(8,128)(2,1)S(1)} %get-tuple-element.28), channel_id=1, source_target_pairs={{0,14},{2,0},{4,2},{6,4},{8,6},{10,8},{12,10},{14,12},{16,30},{18,... | collective-permute-start | bytes 786440 | tf_op jit(solution)/shard_map/ppermute | solution.py:355
  66.5 82.0 %collective-permute-start.7 = (bf16[2,128,512]{2,1,0:T(8,128)(2,1)S(1)}, bf16[2,128,512]{2,1,0:T(8,128)(2,1)S(1)}, u32[]{:S(2)}, u32[]{:S(2)}) collective-permute-start(bf16[2,128,512]{2,1,0:T(8,128)(2,1)S(1)} %get-tuple-element.29), channel_id=1, source_target_pairs={{0,12},{2,14},{4,0},{6,2},{8,4},{10,6},{12,8},{14,10},{16,28},{18,... | collective-permute-start | bytes 786440 | tf_op jit(solution)/shard_map/ppermute | solution.py:355
  74.8 64.7 %collective-permute-start.5 = (bf16[2,128,512]{2,1,0:T(8,128)(2,1)S(1)}, bf16[2,128,512]{2,1,0:T(8,128)(2,1)S(1)}, u32[]{:S(2)}, u32[]{:S(2)}) collective-permute-start(bf16[2,128,512]{2,1,0:T(8,128)(2,1)S(1)} %get-tuple-element.31), channel_id=1, source_target_pairs={{0,8},{2,10},{4,12},{6,14},{8,0},{10,2},{12,4},{14,6},{16,24},{18,... | collective-permute-start | bytes 786440 | tf_op jit(solution)/shard_map/ppermute | solution.py:355
  138.3 10.1 %collective-permute-start.6 = (bf16[2,128,512]{2,1,0:T(8,128)(2,1)S(1)}, bf16[2,128,512]{2,1,0:T(8,128)(2,1)S(1)}, u32[]{:S(2)}, u32[]{:S(2)}) collective-permute-start(bf16[2,128,512]{2,1,0:T(8,128)(2,1)S(1)} %get-tuple-element.30), channel_id=1, source_target_pairs={{0,10},{2,12},{4,14},{6,0},{8,2},{10,4},{12,6},{14,8},{16,26},{18,... | collective-permute-start | bytes 786440 | tf_op jit(solution)/shard_map/ppermute | solution.py:355
  148.6 1.3 copy-start.4
  149.9 39.0 %copy-start.2 = (s32[512]{0:T(512)S(1)}, s32[512]{0:T(512)}, u32[]{:S(2)}) copy-start(s32[512]{0:T(512)} %param.9) | copy-start | bytes 6148
  193.8 2.7 %collective-permute-start.9 = (f32[4,128,512]{2,1,0:T(8,128)S(1)}, f32[4,128,512]{2,1,0:T(8,128)S(1)}, u32[]{:S(2)}, u32[]{:S(2)}) collective-permute-start(f32[4,128,512]{2,1,0:T(8,128)S(1)} %get-tuple-element.19.refs_0_), channel_id=1, source_target_pairs={{0,1},{1,0},{2,3},{3,2},{4,5},{5,4},{6,7},{7,6},{8,9},{9,8},{10,11... | collective-permute-start | bytes 3145736 | tf_op jit(solution)/shard_map/ppermute | solution.py:373
